TPU v7x, 256 devices: a whole 4x4x8 slice. The times are simulated.
256 devices in a mesh: row: 128 (over x_lo, y, z, core), col: 2 (over x_hi).
Axes of the slice: x: 4 (x_hi: 2, x_lo: 2; x = x_hi * 2 + x_lo), y: 4, z: 8, core: 2. Of those that a mesh axis runs over, the one named last changes fastest.
Arguments:
- row_embed: bfloat16 [300, 131072], P(None, 'row'), may hold values from -1.796875 to 1.796875
- col_embed: bfloat16 [300, 2, 2048], P(None, 'col', 'row'), may hold values from -1.796875 to 1.796875
- counts: int32 [131072, 2, 2048], P('row', 'col'), may hold values from 0 to 64, as said below
- occupancy: int32 [1024, 2, 16], P('row', 'col'), may hold values from 0 to 1, as said below
- row_marg: int32 [131072], P('row'), may hold values from 2000 to 199999
- col_marg: int32 [2, 2048], P('col', 'row'), may hold values from 2000 to 199999
- log_total: float32 [1], replicated, may hold values from 18 to 22
Outputs:
- grad_rows: float32 [300, 131072], P(None, 'row')
- grad_cols: float32 [300, 2, 2048], P(None, 'col', 'row')
Inputs may be any that keep to these rules, and one draw needn't show every extreme that they name: counts of the band's cells; zero in part of the cells. `occupancy`: the share of tiles marked 1 differs from row tile to row tile.
All inputs are finite; a program needn't handle non-finite values.
Results may differ from a plain program's by a relative error of at most 0.0018.
Values may be sent and summed in bfloat16 or wider, within the bound.
No kernel may reach another device: no remote copies, remote signals or barrier semaphores. Data moves between devices by JAX's collectives and lax.ppermute only.
A program may use at most 64 MiB of HBM per device.

v0:
```python
import math

import jax
import jax.numpy as jnp
from jax import lax
from jax.sharding import PartitionSpec as P


def cell_slope(scores, count_piece, log_row, log_piece, log_base):
    count_values = count_piece.astype(jnp.float32)
    log_ratio = jnp.log(jnp.maximum(count_values, 1.0)) + (
        log_base - log_row[:, None] - log_piece[None, :]
    )
    score_gap = scores - log_ratio
    return jnp.where(
        count_piece > 0,
        (0.1 + 0.25 * jnp.sqrt(count_values)) * score_gap,
        jax.nn.sigmoid(score_gap),
    )


def band_residual(row_embed, cols_piece, count_piece, occ_float, log_row, log_piece, log_base):
    piece_width = cols_piece.shape[1]
    row_tiles = occ_float.shape[0]
    band_tiles = occ_float.shape[1]
    tile_size = row_embed.shape[1] // row_tiles
    scores = jnp.einsum("di,dj->ij", row_embed, cols_piece, preferred_element_type=jnp.float32)
    slopes = cell_slope(scores, count_piece, log_row, log_piece, log_base)
    tile_index = jnp.arange(piece_width, dtype=jnp.int32) // tile_size
    selector = (tile_index[None, :] == jnp.arange(band_tiles, dtype=jnp.int32)[:, None]).astype(
        jnp.float32
    )
    col_mask = jnp.dot(occ_float, selector, preferred_element_type=jnp.float32)
    masked = slopes.reshape(row_tiles, tile_size, piece_width) * col_mask[:, None, :]
    return masked.reshape(-1, piece_width).astype(jnp.bfloat16)


def body(row_embed, col_embed, counts, occupancy, row_marg, col_marg, log_total):
    rows_dev = row_embed.shape[1]
    cols_local = col_embed.shape[2]
    total_rows = rows_dev * lax.axis_size("row")
    total_cols = cols_local * lax.axis_size("row") * lax.axis_size("col")
    local_counts = counts[:, 0, :]
    occ_float = occupancy[:, 0, :].astype(jnp.float32)
    log_row = jnp.log(row_marg.astype(jnp.float32))
    log_base = log_total[0]
    marg_shard = col_marg[None]
    gathered, marg_all = (
        lax.all_gather(col_embed, "row", axis=2, tiled=True),
        lax.all_gather(marg_shard, "row", axis=2, tiled=True),
    )
    band_cols = gathered[:, 0, :]
    log_col = jnp.log(marg_all[0, 0].astype(jnp.float32))
    residual = band_residual(
        row_embed, band_cols, local_counts, occ_float, log_row, log_col, log_base
    )
    partial_rows = jnp.einsum("dj,ij->di", band_cols, residual, preferred_element_type=jnp.float32)
    column_term = jnp.einsum("di,ij->dj", row_embed, residual, preferred_element_type=jnp.float32)
    summed_cols = lax.psum_scatter(column_term[:, None, :], "row", scatter_dimension=2, tiled=True)
    summed_rows = lax.psum(partial_rows, "col")
    grad_rows = summed_rows * (1.0 / math.sqrt(total_cols))
    grad_cols = summed_cols * (1.0 / math.sqrt(total_rows))
    return (grad_rows, grad_cols)


def solution(mesh):
    placed = (
        P(None, "row"),
        P(None, "col", "row"),
        P("row", "col", None),
        P("row", "col", None),
        P("row"),
        P("col", "row"),
        P(),
    )
    return jax.shard_map(
        body,
        mesh=mesh,
        in_specs=placed,
        out_specs=(P(None, "row"), P(None, "col", "row")),
        check_vma=False,
    )
```

profile of v0, /device:TPU:1, one launch (start us, length us, event | category | flops | bytes accessed | tf_op | source)
XLA Modules:
  0.0 1400.7 jit_solution(6107628418544211194)
XLA Ops:
  7.2 0.0 copy-start
  7.2 0.0 all-gather.3.cloned.1.call-start
  7.2 0.7 all-gather.3.cloned.1.call-update
  7.9 0.0 all-reduce.5.cloned.1.call-start
  8.6 1.3 fusion.15
  10.6 0.8 bitcast_dynamic-update-slice_fusion
  11.4 23.9 %all-reduce = s32[2048]{0:T(1024)S(1)} all-reduce(s32[2048]{0:T(1024)S(1)} %bitcast_dynamic-update-slice_fusion), channel_id=2, replica_groups=mesh['row'=128,'col'=2] {'row'}, use_global_device_ids=true, to_apply=%add | all-reduce | flops 2048 | bytes 16384
  35.3 0.7 log_subtract_fusion
  36.0 0.8 convolution_bitcast_fusion.1
  36.8 188.5 %all-gather.3.cloned.1.call-done = bf16[300,1,2048]{0,2,1:T(8,128)(2,1)} async-done(((bf16[300,1,16]{0,2,1:T(8,128)(2,1)}), bf16[300,1,2048]{0,2,1:T(8,128)(2,1)}) %all-gather.3.cloned.1.call-update) | async-done | bytes 1228816 | tf_op jit(solution)/shard_map/all_gather | solution.py:49
  225.4 0.0 copy-done
  225.4 0.0 copy-start.2
  225.4 13.3 fusion
  238.7 0.0 copy-start.1
  238.7 1.9 copy-done.1
  240.6 0.0 copy-done.2
  240.6 2.6 fusion.6
  243.2 0.0 all-reduce.5.cloned.1.call-update
  243.2 0.0 all-reduce.7.cloned.1.call-start
  243.3 3.6 convolution_bitcast_fusion
  246.9 5.5 copy.16
  252.5 0.0 all-reduce.7.cloned.1.call-update
  253.1 47.0 %all-reduce.5.cloned.1.call-done = f32[300,1024]{1,0:T(8,128)} async-done(((f32[300,1024]{1,0:T(8,128)}), f32[300,1024]{1,0:T(8,128)}) %all-reduce.5.cloned.1.call-update) | async-done | bytes 1228816 | tf_op jit(solution)/shard_map/psum | solution.py:60
  300.1 2.5 broadcast_multiply_fusion
  302.6 1090.2 %all-reduce.7.cloned.1.call-done = f32[300,1,2048]{0,1,2:T(1,128)} async-done(((f32[300,1,2048]{0,1,2:T(1,128)}), f32[300,1,2048]{0,1,2:T(1,128)}) %all-reduce.7.cloned.1.call-update) | async-done | bytes 2457616
  1392.8 0.8 dynamic-slice_multiply_fusion
  1393.6 0.6 copy.17
  (3 shorter events, 0.0 us)
Async XLA Ops:
  7.2 218.2 %copy-start = (bf16[300,1024]{1,0:T(8,128)(2,1)S(1)}, bf16[300,1024]{1,0:T(8,128)(2,1)}, u32[]{:S(2)}) copy-start(bf16[300,1024]{1,0:T(8,128)(2,1)} %param.7) | copy-start | bytes 1843204
  7.2 218.2 %all-gather.3.cloned.1.call-start = ((), (), s32[]{:S(2)}) async-start(), calls=%async_computation | async-start | bytes 1585152 | tf_op jit(solution)/shard_map/all_gather | solution.py:49
  7.9 292.2 %all-reduce.5.cloned.1.call-start = ((), (), s32[]{:S(2)}) async-start(), calls=%async_computation.1 | async-start | bytes 2490368 | tf_op jit(solution)/shard_map/psum | solution.py:60
  225.4 15.3 %copy-start.2 = (bf16[300,1,2048]{0,2,1:T(8,128)(2,1)S(1)}, bf16[300,1,2048]{0,2,1:T(8,128)(2,1)}, u32[]{:S(2)}) copy-start(bf16[300,1,2048]{0,2,1:T(8,128)(2,1)} %all-gather.3.cloned.1.call-done) | copy-start | bytes 3686404
  238.7 1.9 copy-start.1
  243.2 1149.6 %all-reduce.7.cloned.1.call-start = ((), (), s32[]{:S(2)}) async-start(), calls=%async_computation.2 | async-start | bytes 6291456
Sparse Core Ops, SparseCore 0:
  9.9 215.4 all-gather.2
  243.4 56.7 all-reduce.4
  302.9 1089.8 all-reduce.6
where the time goes:
time: 1400 us
  waiting for transfers between devices  1330 us (95%)
  blocking collectives  23.9 us (2%)
  matrix products  20.4 us (1%)
  between operations  15.8 us (1%)
    unnamed x4, waiting for transfers between devices  1090 us
    all_gather x1, waiting for transfers between devices, body(): lax.all_gather(col_embed, 'row', axis=2, tiled=True)  189 us
    psum x1, waiting for transfers between devices, body(): summed_rows = lax.psum(partial_rows, 'col')  47 us
  transfers between devices with their start and end apart: 3, of which 3 were waited for; matrix products, arithmetic and copies ran while one was open for 1% of the time, Pallas kernels for 0%

commit v1 on v0

v1 whole, which is shorter than its diff:
```python
import functools
import math

import jax
import jax.numpy as jnp
from jax import lax
from jax.experimental import pallas as pl
from jax.experimental.pallas import tpu as pltpu
from jax.sharding import Mesh, PartitionSpec as P

SPLIT = (2, 4, 8, 2, 2)
AXES = ("xl", "y", "z", "core", "xh")
ROW = ("xl", "y", "z", "core")
TILE = 128
WIDE = 384
BLOCK = 256
PACK = 40
VMEM_LIMIT = 32 * 1024 * 1024
HALF_LIMIT = 48 * 1024 * 1024
SWAP = [(0, 1), (1, 0)]


def three_parts(values):
    high = values.astype(jnp.bfloat16).astype(jnp.float32)
    rest = values - high
    middle = rest.astype(jnp.bfloat16).astype(jnp.float32)
    return high, middle, rest - middle


def prep_cols(embed_ref, marg_ref, out_ref):
    copies, words, wide = out_ref.shape
    depth = embed_ref.shape[1]
    log_col = jnp.log(marg_ref[...].astype(jnp.float32))
    square = (words, words)
    same = lax.broadcasted_iota(jnp.int32, square, 0) == lax.broadcasted_iota(jnp.int32, square, 1)
    spread = jnp.where(same, jnp.broadcast_to(log_col, square), 0.0).sum(axis=1, keepdims=True)
    high, middle, low = three_parts(spread)
    lane = lax.broadcasted_iota(jnp.int32, (words, wide - 256), 1) + 256
    tail = jnp.where(lane == depth, high, 0.0)
    tail = jnp.where(lane == depth + 1, middle, tail)
    tail = jnp.where(lane == depth + 2, low, tail)
    tail = jnp.where((lane >= depth + 3) & (lane < depth + 6), 1.0, tail)
    embed = embed_ref[...].astype(jnp.float32)
    padded = jnp.concatenate([embed, jnp.zeros((words, wide - depth), jnp.float32)], axis=1)
    block = jnp.concatenate([padded[:, :256], padded[:, 256:] + tail], axis=1).astype(jnp.bfloat16)
    for copy in range(copies):
        out_ref[copy] = block


def prep_rows(embed_ref, marg_ref, total_ref, wide_ref, turned_ref):
    depth, rows = embed_ref.shape
    wide = wide_ref.shape[0]
    log_row = jnp.log(marg_ref[...].astype(jnp.float32)) - total_ref[0]
    high, middle, low = three_parts(log_row)
    start = depth - depth % 8
    line = lax.broadcasted_iota(jnp.int32, (wide - start, rows), 0) + start
    tail = jnp.where((line >= depth) & (line < depth + 3), 1.0, 0.0)
    tail = jnp.where(line == depth + 3, high, tail)
    tail = jnp.where(line == depth + 4, middle, tail)
    tail = jnp.where(line == depth + 5, low, tail)
    embed = embed_ref[...].astype(jnp.float32)
    padded = jnp.concatenate([embed, jnp.zeros((wide - depth, rows), jnp.float32)], axis=0)
    whole = jnp.concatenate([padded[:start], padded[start:] + tail], axis=0)
    wide_ref[...] = whole.astype(jnp.bfloat16)
    turned_ref[...] = whole.T.astype(jnp.bfloat16)


def half_step(first, place, occ_ref, count_ref, wide_ref, turned_ref, own_ref, peer_ref, *rest):
    if first:
        row_out, keep_ref, send_ref, turned_cols, residual_ref, held, arrived = rest
    else:
        row_in, row_out, keep_ref, send_ref, turned_cols, residual_ref, held, arrived = rest
    which, core = place[0], place[1]
    chips, words, wide = own_ref.shape
    depth_rows = row_out.shape[0]
    rows, width = residual_ref.shape
    tiles = width // TILE
    blocks = rows // BLOCK

    def fetch(step):
        return pltpu.make_async_copy(
            count_ref.at[
                pl.ds(step * BLOCK, BLOCK), pl.ds(pl.multiple_of(which * tiles, tiles), tiles), :
            ],
            held.at[step],
            arrived.at[step],
        )

    for step in range(blocks):
        fetch(step).start()

    own, peer = own_ref[...], peer_ref[...]
    low = jnp.where(core == 0, own, peer)
    high = jnp.where(core == 0, peer, own)
    pair = jnp.concatenate([low[:, None], high[:, None]], axis=1)
    turned_cols[...] = pair.reshape(width, wide).T
    @pl.loop(0, blocks)
    def _(step):
        fetch(step).wait()
        count_flat = held.at[step].reshape(BLOCK * tiles, TILE)
        row_block = turned_ref[pl.ds(pl.multiple_of(step * BLOCK, BLOCK), BLOCK), :]
        for chunk in range(width // 256):
            cols = turned_cols[:, chunk * 256 : (chunk + 1) * 256]
            gap_base = jnp.dot(row_block, cols, preferred_element_type=jnp.float32)
            parts = []
            for side in range(2):
                tile = chunk * 2 + side
                cnt = count_flat[pl.ds(tile, BLOCK, stride=tiles), :]
                at_least = jnp.maximum(cnt.astype(jnp.float32), 1.0)
                gap = gap_base[:, side * TILE : (side + 1) * TILE] - jnp.log(at_least)
                slope = jnp.where(
                    cnt > 0,
                    (0.1 + 0.25 * (at_least * lax.rsqrt(at_least))) * gap,
                    1.0 / (1.0 + jnp.exp(-gap)),
                )
                pieces = []
                for sub in range(BLOCK // TILE):
                    mark = occ_ref[step * (BLOCK // TILE) + sub, which * tiles + tile]
                    pieces.append(slope[sub * TILE : (sub + 1) * TILE] * mark.astype(jnp.float32))
                parts.append(jnp.concatenate(pieces, axis=0).astype(jnp.bfloat16))
            residual_ref[
                pl.ds(pl.multiple_of(step * BLOCK, BLOCK), BLOCK), chunk * 256 : (chunk + 1) * 256
            ] = jnp.concatenate(parts, axis=1)

    row_total = lax.dot_general(
        turned_cols[:depth_rows, :], residual_ref[...], (((1,), (1,)), ((), ())),
        preferred_element_type=jnp.float32,
    )
    if not first:
        row_total = row_total + row_in[...]
    row_out[...] = row_total.astype(row_out.dtype)
    col_sum = jnp.dot(
        wide_ref[:depth_rows, :], residual_ref[...], preferred_element_type=jnp.float32
    )
    filled = jnp.concatenate([col_sum, jnp.zeros((wide - depth_rows, width), jnp.float32)], axis=0)
    words_first = filled.T.reshape(chips, 2, 2, 8, wide)
    lane = lax.broadcasted_iota(jnp.int32, (8, TILE), 1)
    for chip in range(chips):
        packed = []
        for side in range(2):
            block = words_first[chip, side]
            last = jnp.where(
                lane < 64, block[0, :, 256:], pltpu.roll(block[1, :, 256:], 64, 1)
            )
            packed.append(
                jnp.concatenate(
                    [block[0, :, :128], block[1, :, :128], block[0, :, 128:256],
                     block[1, :, 128:256], last], axis=0)
            )
        keep_ref[chip] = jnp.where(core == 0, packed[0], packed[1])
        send_ref[chip] = jnp.where(core == 0, packed[1], packed[0])


def run_half(first, place, occ, count_view, wide_rows, turned_rows, own, peer, row_in):
    rows = turned_rows.shape[0]
    chips, words, wide = own.shape
    width = chips * 2 * words
    depth_rows = 304
    smem = pl.BlockSpec(memory_space=pltpu.SMEM)
    vmem = pl.BlockSpec(memory_space=pltpu.VMEM)
    operands = [place, occ, count_view, wide_rows, turned_rows, own, peer]
    if not first:
        operands.append(row_in)
    chunk = jax.ShapeDtypeStruct((chips, PACK, TILE), jnp.float32)
    return pl.pallas_call(
        functools.partial(half_step, first),
        in_specs=[smem, smem, pl.BlockSpec(memory_space=pltpu.HBM)] + [vmem] * (len(operands) - 3),
        out_specs=[vmem] * 3,
        scratch_shapes=[
            pltpu.VMEM((wide, width), jnp.bfloat16),
            pltpu.VMEM((rows, width), jnp.bfloat16),
            pltpu.VMEM((rows // BLOCK, BLOCK, width // TILE, TILE), jnp.int32),
            pltpu.SemaphoreType.DMA((rows // BLOCK,)),
        ],
        out_shape=[
            jax.ShapeDtypeStruct((depth_rows, rows), jnp.float32 if first else jnp.bfloat16),
            chunk,
            chunk,
        ],
        compiler_params=pltpu.CompilerParams(vmem_limit_bytes=HALF_LIMIT),
        cost_estimate=pl.CostEstimate(
            flops=6 * rows * width * 300, bytes_accessed=8 * rows * width // 2,
            transcendentals=rows * width,
        ),
    )(*operands)


def join(place, keep_a, got_a, keep_b, got_b, out_ref):
    chips = keep_a.shape[0]
    which = place[0]
    for at, keep, got in ((which, keep_a, got_a), (1 - which, keep_b, got_b)):
        for chip in range(chips):
            out_ref[at * chips + chip] = (keep[chip] + got[chip]).astype(jnp.bfloat16)


def finish(row_scale, col_scale, mine_ref, theirs_ref, got_ref, rows_ref, cols_ref):
    depth = rows_ref.shape[0]
    both = mine_ref[...].astype(jnp.float32) + theirs_ref[...].astype(jnp.float32)
    rows_ref[...] = both[:depth] * row_scale
    total = got_ref[...].astype(jnp.float32).sum(axis=0) * col_scale
    last = total[32:40]
    turned = pltpu.roll(last, 64, 1)
    cols_ref[0:8, :] = jnp.concatenate([total[0:8], total[16:24], last], axis=1)[:, :depth]
    cols_ref[8:16, :] = jnp.concatenate([total[8:16], total[24:32], turned], axis=1)[:, :depth]


def body(row_embed, col_embed, counts, occupancy, row_marg, col_marg, log_total):


    depth, rows = row_embed.shape
    words = col_embed.shape[2]
    core = lax.axis_index("core")
    xl = lax.axis_index("xl")
    params = pltpu.CompilerParams(vmem_limit_bytes=VMEM_LIMIT)
    smem = pl.BlockSpec(memory_space=pltpu.SMEM)
    vmem = pl.BlockSpec(memory_space=pltpu.VMEM)

    fan_out = pl.pallas_call(
        prep_cols,
        out_shape=jax.ShapeDtypeStruct((32, words, WIDE), jnp.bfloat16),
        compiler_params=params,
    )(col_embed[:, 0, :].T, col_marg)
    quarter = lax.all_to_all(fan_out, ("y", "z"), 0, 0, tiled=True)
    wide_rows, turned_rows = pl.pallas_call(
        prep_rows,
        in_specs=[vmem, vmem, smem],
        out_shape=[
            jax.ShapeDtypeStruct((WIDE, rows), jnp.bfloat16),
            jax.ShapeDtypeStruct((rows, WIDE), jnp.bfloat16),
        ],
        compiler_params=params,
        cost_estimate=pl.CostEstimate(flops=rows * WIDE, bytes_accessed=4 * rows * WIDE, transcendentals=0),
    )(row_embed, row_marg[None, :], log_total)
    count_view = counts.reshape(rows, 16, TILE)
    occ = occupancy[:, 0, :]

    peer = lax.ppermute(quarter, "core", SWAP)
    far = lax.ppermute(quarter, "xl", SWAP)
    far_peer = lax.ppermute(far, "core", SWAP)
    row_part, keep_a, send_a = run_half(
        True, jnp.stack([xl, core]), occ, count_view, wide_rows, turned_rows, quarter, peer, None
    )
    got_a = lax.ppermute(send_a, "core", SWAP)
    mine, keep_b, send_b = run_half(
        False, jnp.stack([1 - xl, core]), occ, count_view, wide_rows, turned_rows, far, far_peer,
        row_part,
    )
    got_b = lax.ppermute(send_b, "core", SWAP)
    theirs = lax.ppermute(mine, "xh", SWAP)

    outgoing = pl.pallas_call(
        join,
        in_specs=[smem, vmem, vmem, vmem, vmem],
        out_shape=jax.ShapeDtypeStruct((64, PACK, TILE), jnp.bfloat16),
        compiler_params=params,
    )(xl[None], keep_a, got_a, keep_b, got_b)
    arrived = lax.all_to_all(outgoing, ("xl", "y", "z"), 0, 0, tiled=True)
    grad_rows, grad_cols = pl.pallas_call(
        functools.partial(finish, 1.0 / math.sqrt(words * 256), 1.0 / math.sqrt(rows * 128)),
        in_specs=[vmem, vmem, vmem],
        out_specs=[vmem, vmem],
        out_shape=[
            jax.ShapeDtypeStruct((depth, rows), jnp.float32),
            jax.ShapeDtypeStruct((words, depth), jnp.float32),
        ],
        compiler_params=params,
    )(mine, theirs, arrived)
    return (grad_rows, grad_cols.T[:, None, :])


def solution(mesh):
    fine = Mesh(mesh.devices.reshape(SPLIT), AXES)
    placed = (
        P(None, ROW),
        P(None, "xh", ROW),
        P(ROW, "xh", None),
        P(ROW, "xh", None),
        P(ROW),
        P("xh", ROW),
        P(),
    )
    return jax.shard_map(
        body,
        mesh=fine,
        in_specs=placed,
        out_specs=(P(None, ROW), P(None, "xh", ROW)),
        check_vma=False,
    )
```

time: 1400 us -> 89.3 us (0.06)
  waiting for transfers between devices: 1330 us -> 22.8 us
  starting transfers between devices: 0.12 us -> 22.1 us
  matrix products: 20.4 us -> 0 us
  Pallas kernels: 0 us -> 16.9 us
  between operations: 15.8 us -> 1.39 us
    unnamed x4 -> x0, waiting for transfers between devices: 1090 us -> none
    all_gather x1 -> x0, waiting for transfers between devices: 189 us -> none  [body(): lax.all_gather(col_embed, 'row', axis=2, tiled=True)]
    psum x1 -> x0, waiting for transfers between devices: 47 us -> none  [body(): summed_rows = lax.psum(partial_rows, 'col')]
    unnamed x1 -> x0, blocking collectives: 23.9 us -> none
    all_to_all x0 -> x1, blocking collectives: none -> 23.5 us  [body(): quarter = lax.all_to_all(fan_out, ('y', 'z'), 0, 0, tiled=True)]
    ppermute x0 -> x6, waiting for transfers between devices: none -> 22.8 us  [the longest x1 21.1 us: body(): theirs = lax.ppermute(mine, 'xh', SWAP)]
    dot_general x4 -> x0, matrix products: 20.4 us -> none  [the longest x1 13.3 us: band_residual(): jnp.einsum('di,dj->ij', row_embed, cols_piece, preferred_element_type=jnp...]
    pallas_call x0 -> x6, Pallas kernels: none -> 16.9 us  [the longest x2 14 us: run_half(): pl.pallas_call(functools.partial(half_step, first), in_specs=[smem, smem,...]
  transfers between devices with their start and end apart: 3 -> 7, of which waited for: 3 -> 2; matrix products, arithmetic and copies ran while one was open for 1% -> 0% of each run, Pallas kernels for 0% -> 16%
where the time goes in v1:
time: 89.3 us; the launch traced here: 88.9 us
  blocking collectives  23.5 us (26%)
  waiting for transfers between devices  22.8 us (26%)
  starting transfers between devices  22.1 us (25%)
  Pallas kernels  16.9 us (19%)
  local copies, waits for them, and re-layouts  2.11 us (2%)
  between operations  1.39 us (2%)
    all_to_all x1, blocking collectives, body(): quarter = lax.all_to_all(fan_out, ('y', 'z'), 0, 0, tiled=True)  23.5 us
    ppermute x1, waiting for transfers between devices, body(): theirs = lax.ppermute(mine, 'xh', SWAP)  21.1 us
    pallas_call x2, Pallas kernels, run_half(): pl.pallas_call(functools.partial(half_step, first), in_specs=[smem, smem,...  14 us
    all_to_all x1, starting transfers between devices, body(): arrived = lax.all_to_all(outgoing, ('xl', 'y', 'z'), 0, 0, tiled=True)  8.94 us
    ppermute x1, starting transfers between devices, body(): far_peer = lax.ppermute(far, 'core', SWAP)  4.63 us
    ppermute x1, starting transfers between devices, body(): peer = lax.ppermute(quarter, 'core', SWAP)  4.12 us
    ppermute x1, starting transfers between devices, body(): theirs = lax.ppermute(mine, 'xh', SWAP)  2.53 us
    unnamed x10, local copies, waits for them, and re-layouts  2.11 us
  transfers between devices with their start and end apart: 7, of which 2 were waited for; matrix products, arithmetic and copies ran while one was open for 0% of the time, Pallas kernels for 16%

profile of v1, /device:TPU:1, one launch (start us, length us, event | category | flops | bytes accessed | tf_op | source)
XLA Modules:
  0.0 88.9 jit_solution(8213891479579655877)
XLA Ops:
  0.6 0.0 copy-start
  0.6 0.0 copy-start.1
  0.7 0.0 copy-start.2
  0.7 0.8 copy-done.2
  1.4 0.0 copy-start.4
  1.4 0.7 copy-done.4
  2.1 0.1 shard_map.87
  2.2 23.5 %all_to_all.10.own_ref = bf16[32,16,384]{2,1,0:T(8,128)(2,1)S(1)} all-to-all(bf16[32,16,384]{2,1,0:T(8,128)(2,1)S(1)} %shard_map.87), channel_id=1, replica_groups=mesh['xl'=2,'y'=4,'z'=8,'core'=2,'xh'=2] {'y','z'}, dimensions={0} | all-to-all | bytes 786432 | tf_op jit(solution)/shard_map/all_to_all | solution.py:223
  25.7 1.2 %collective-permute-start = (bf16[32,16,384]{2,1,0:T(8,128)(2,1)S(1)}, bf16[32,16,384]{2,1,0:T(8,128)(2,1)S(1)}, u32[]{:S(2)}, u32[]{:S(2)}) collective-permute-start(bf16[32,16,384]{2,1,0:T(8,128)(2,1)S(1)} %all_to_all.10.own_ref), channel_id=1, source_target_pairs={{0,128},{128,0},{1,129},{129,1},{2,130},{130,2},{3,131},{131,3},{4... | collective-permute-start | bytes 1179656 | tf_op jit(solution)/shard_map/ppermute | solution.py:238
  26.9 4.1 %collective-permute-start.2 = (bf16[32,16,384]{2,1,0:T(8,128)(2,1)S(1)}, bf16[32,16,384]{2,1,0:T(8,128)(2,1)S(1)}, u32[]{:S(2)}, u32[]{:S(2)}) collective-permute-start(bf16[32,16,384]{2,1,0:T(8,128)(2,1)S(1)} %all_to_all.10.own_ref), channel_id=1, source_target_pairs={{0,2},{2,0},{1,3},{3,1},{4,6},{6,4},{5,7},{7,5},{8,10},{10,8},{9,1... | collective-permute-start | bytes 1179656 | tf_op jit(solution)/shard_map/ppermute | solution.py:237
  31.7 0.0 copy-done
  31.7 0.0 copy-start.3
  31.7 0.7 copy-done.3
  32.4 0.3 shard_map.86
  32.7 0.0 collective-permute-done.own_ref
  32.7 4.6 %collective-permute-start.1 = (bf16[32,16,384]{2,1,0:T(8,128)(2,1)S(1)}, bf16[32,16,384]{2,1,0:T(8,128)(2,1)S(1)}, u32[]{:S(2)}, u32[]{:S(2)}) collective-permute-start(bf16[32,16,384]{2,1,0:T(8,128)(2,1)S(1)} %collective-permute-done.own_ref), channel_id=1, source_target_pairs={{0,2},{2,0},{1,3},{3,1},{4,6},{6,4},{5,7},{7,5},{8,10},{10,8},{9,1... | collective-permute-start | bytes 1179656 | tf_op jit(solution)/shard_map/ppermute | solution.py:239
  37.3 0.1 pad_add_fusion.place
  37.4 0.1 pad_add_fusion.1.place
  37.4 0.0 collective-permute-done.2.peer_ref
  37.4 0.0 copy-done.1
  37.4 7.0 %shard_map.88 = (f32[304,1024]{1,0:T(8,128)S(1)}, f32[32,40,128]{2,1,0:T(8,128)S(1)}, f32[32,40,128]{2,1,0:T(8,128)S(1)}) custom-call(s32[2]{0:T(128)S(1)} %pad_add_fusion.1.place, s32[8,16]{1,0:T(8,128)S(1)} %bitcast.12, s32[1024,16,128]{2,1,0:T(8,128)} %bitcast.16, bf16[384,1024]{1,0:T(8,128)(2,1)S(1)} %get-tuple-element.12.wide_ref, ...), custom_call_target="tpu_custom_call" | custom-call | flops 1887436800 | bytes 4194304 | tf_op jit(solution)/shard_map/pallas_call | solution.py:165
  44.5 0.1 collective-permute-start.4
  44.6 0.0 collective-permute-done.1.peer_ref
  44.6 7.0 %shard_map.89 = (bf16[304,1024]{1,0:T(8,128)(2,1)S(1)}, f32[32,40,128]{2,1,0:T(8,128)S(1)}, f32[32,40,128]{2,1,0:T(8,128)S(1)}) custom-call(s32[2]{0:T(128)S(1)} %pad_add_fusion.place, s32[8,16]{1,0:T(8,128)S(1)} %bitcast.13, s32[1024,16,128]{2,1,0:T(8,128)} %bitcast.17, bf16[384,1024]{1,0:T(8,128)(2,1)S(1)} %get-tuple-element.12.wide_ref, ...), custom_call_target="tpu_custom_call" | custom-call | flops 1887436800 | bytes 4194304 | tf_op jit(solution)/shard_map/pallas_call | solution.py:165
  51.6 0.6 collective-permute-start.5
  52.2 0.0 collective-permute-done.4.got_a
  52.2 1.7 %collective-permute-done.5.got_b = f32[32,40,128]{2,1,0:T(8,128)S(1)} collective-permute-done((f32[32,40,128]{2,1,0:T(8,128)S(1)}, f32[32,40,128]{2,1,0:T(8,128)S(1)}, u32[]{:S(2)}, u32[]{:S(2)}) %collective-permute-start.5) | collective-permute-done | bytes 655392 | tf_op jit(solution)/shard_map/ppermute | solution.py:248
  53.9 1.0 %shard_map.90 = bf16[64,40,128]{2,1,0:T(8,128)(2,1)} custom-call(s32[1]{0:T(128)} %bitcast.7.place, f32[32,40,128]{2,1,0:T(8,128)S(1)} %get-tuple-element.16.keep_a, f32[32,40,128]{2,1,0:T(8,128)S(1)} %collective-permute-done.4.got_a, f32[32,40,128]{2,1,0:T(8,128)S(1)} %get-tuple-element.18.keep_b, f32[32,40,128]{2,1,0:T(8,128)S(1)} %collective-permute-done.5.got_b), custom_call_target="tpu_custom_call" | custom-call | tf_op jit(solution)/shard_map/pallas_call | solution.py:251
  54.9 8.9 %all-to-all-start.1 = ((bf16[64,40,128]{2,1,0:T(8,128)(2,1)}), bf16[64,40,128]{2,1,0:T(8,128)(2,1)S(1)}, u32[]{:S(2)}, u32[]{:S(2)}) async-start(bf16[64,40,128]{2,1,0:T(8,128)(2,1)} %shard_map.90), calls=%async_computation.1 | async-start | bytes 1310720 | tf_op jit(solution)/shard_map/all_to_all | solution.py:257
  63.8 2.5 %collective-permute-start.3 = (bf16[304,1024]{1,0:T(8,128)(2,1)S(1)}, bf16[304,1024]{1,0:T(8,128)(2,1)S(1)}, u32[]{:S(2)}, u32[]{:S(2)}) collective-permute-start(bf16[304,1024]{1,0:T(8,128)(2,1)S(1)} %get-tuple-element.15.mine_ref), channel_id=1, source_target_pairs={{0,1},{1,0},{2,3},{3,2},{4,5},{5,4},{6,7},{7,6},{8,9},{9,8},{10,11... | collective-permute-start | bytes 1867784 | tf_op jit(solution)/shard_map/ppermute | solution.py:249
  66.3 21.1 %collective-permute-done.3.theirs_ref = bf16[304,1024]{1,0:T(8,128)(2,1)S(1)} collective-permute-done((bf16[304,1024]{1,0:T(8,128)(2,1)S(1)}, bf16[304,1024]{1,0:T(8,128)(2,1)S(1)}, u32[]{:S(2)}, u32[]{:S(2)}) %collective-permute-start.3) | collective-permute-done | bytes 622624 | tf_op jit(solution)/shard_map/ppermute | solution.py:249
  87.5 0.0 all-to-all-done.1.got_ref
  87.5 1.5 %shard_map.91 = (f32[300,1024]{1,0:T(8,128)}, f32[16,300]{1,0:T(8,128)}) custom-call(bf16[304,1024]{1,0:T(8,128)(2,1)S(1)} %get-tuple-element.15.mine_ref, bf16[304,1024]{1,0:T(8,128)(2,1)S(1)} %collective-permute-done.3.theirs_ref, bf16[64,40,128]{2,1,0:T(8,128)(2,1)S(1)} %all-to-all-done.1.got_ref), custom_call_target="tpu_custom_call" | custom-call | tf_op jit(solution)/shard_map/pallas_call | solution.py:258
Async XLA Ops:
  0.6 31.0 %copy-start = (bf16[300,1024]{1,0:T(8,128)(2,1)S(1)}, bf16[300,1024]{1,0:T(8,128)(2,1)}, u32[]{:S(2)}) copy-start(bf16[300,1024]{1,0:T(8,128)(2,1)} %embed_ref.1) | copy-start | bytes 1843204
  0.6 36.8 %copy-start.1 = (s32[8,1,16]{2,1,0:T(1,128)S(1)}, s32[8,1,16]{2,1,0:T(1,128)}, u32[]{:S(2)}) copy-start(s32[8,1,16]{2,1,0:T(1,128)} %param.10) | copy-start | bytes 1540
  0.7 0.8 copy-start.2
  1.4 0.7 copy-start.4
  25.7 7.0 %collective-permute-start = (bf16[32,16,384]{2,1,0:T(8,128)(2,1)S(1)}, bf16[32,16,384]{2,1,0:T(8,128)(2,1)S(1)}, u32[]{:S(2)}, u32[]{:S(2)}) collective-permute-start(bf16[32,16,384]{2,1,0:T(8,128)(2,1)S(1)} %all_to_all.10.own_ref), channel_id=1, source_target_pairs={{0,128},{128,0},{1,129},{129,1},{2,130},{130,2},{3,131},{131,3},{4... | collective-permute-start | bytes 1179656 | tf_op jit(solution)/shard_map/ppermute | solution.py:238
  26.9 10.6 %collective-permute-start.2 = (bf16[32,16,384]{2,1,0:T(8,128)(2,1)S(1)}, bf16[32,16,384]{2,1,0:T(8,128)(2,1)S(1)}, u32[]{:S(2)}, u32[]{:S(2)}) collective-permute-start(bf16[32,16,384]{2,1,0:T(8,128)(2,1)S(1)} %all_to_all.10.own_ref), channel_id=1, source_target_pairs={{0,2},{2,0},{1,3},{3,1},{4,6},{6,4},{5,7},{7,5},{8,10},{10,8},{9,1... | collective-permute-start | bytes 1179656 | tf_op jit(solution)/shard_map/ppermute | solution.py:237
  31.7 0.7 copy-start.3
  32.7 11.9 %collective-permute-start.1 = (bf16[32,16,384]{2,1,0:T(8,128)(2,1)S(1)}, bf16[32,16,384]{2,1,0:T(8,128)(2,1)S(1)}, u32[]{:S(2)}, u32[]{:S(2)}) collective-permute-start(bf16[32,16,384]{2,1,0:T(8,128)(2,1)S(1)} %collective-permute-done.own_ref), channel_id=1, source_target_pairs={{0,2},{2,0},{1,3},{3,1},{4,6},{6,4},{5,7},{7,5},{8,10},{10,8},{9,1... | collective-permute-start | bytes 1179656 | tf_op jit(solution)/shard_map/ppermute | solution.py:239
  44.5 7.7 %collective-permute-start.4 = (f32[32,40,128]{2,1,0:T(8,128)S(1)}, f32[32,40,128]{2,1,0:T(8,128)S(1)}, u32[]{:S(2)}, u32[]{:S(2)}) collective-permute-start(f32[32,40,128]{2,1,0:T(8,128)S(1)} %get-tuple-element.17), channel_id=1, source_target_pairs={{0,2},{2,0},{1,3},{3,1},{4,6},{6,4},{5,7},{7,5},{8,10},{10,8},{9,1... | collective-permute-start | bytes 1966088 | tf_op jit(solution)/shard_map/ppermute | solution.py:243
  51.6 2.3 %collective-permute-start.5 = (f32[32,40,128]{2,1,0:T(8,128)S(1)}, f32[32,40,128]{2,1,0:T(8,128)S(1)}, u32[]{:S(2)}, u32[]{:S(2)}) collective-permute-start(f32[32,40,128]{2,1,0:T(8,128)S(1)} %get-tuple-element.19), channel_id=1, source_target_pairs={{0,2},{2,0},{1,3},{3,1},{4,6},{6,4},{5,7},{7,5},{8,10},{10,8},{9,1... | collective-permute-start | bytes 1966088 | tf_op jit(solution)/shard_map/ppermute | solution.py:248
  54.9 32.6 %all-to-all-start.1 = ((bf16[64,40,128]{2,1,0:T(8,128)(2,1)}), bf16[64,40,128]{2,1,0:T(8,128)(2,1)S(1)}, u32[]{:S(2)}, u32[]{:S(2)}) async-start(bf16[64,40,128]{2,1,0:T(8,128)(2,1)} %shard_map.90), calls=%async_computation.1 | async-start | bytes 1310720 | tf_op jit(solution)/shard_map/all_to_all | solution.py:257
  63.8 23.6 %collective-permute-start.3 = (bf16[304,1024]{1,0:T(8,128)(2,1)S(1)}, bf16[304,1024]{1,0:T(8,128)(2,1)S(1)}, u32[]{:S(2)}, u32[]{:S(2)}) collective-permute-start(bf16[304,1024]{1,0:T(8,128)(2,1)S(1)} %get-tuple-element.15.mine_ref), channel_id=1, source_target_pairs={{0,1},{1,0},{2,3},{3,2},{4,5},{5,4},{6,7},{7,6},{8,9},{9,8},{10,11... | collective-permute-start | bytes 1867784 | tf_op jit(solution)/shard_map/ppermute | solution.py:249

commit v2 on v1

--- a/solution.py
+++ b/solution.py
@@ -15,7 +15,7 @@
 WIDE = 384
 BLOCK = 256
 PACK = 40
-VMEM_LIMIT = 32 * 1024 * 1024
+VMEM_LIMIT = 24 * 1024 * 1024
 HALF_LIMIT = 48 * 1024 * 1024
 SWAP = [(0, 1), (1, 0)]
 
@@ -28,23 +28,37 @@
 
 
 def prep_cols(embed_ref, marg_ref, out_ref):
-    copies, words, wide = out_ref.shape
-    depth = embed_ref.shape[1]
+    copies = out_ref.shape[0]
+    words, depth = embed_ref.shape
     log_col = jnp.log(marg_ref[...].astype(jnp.float32))
     square = (words, words)
     same = lax.broadcasted_iota(jnp.int32, square, 0) == lax.broadcasted_iota(jnp.int32, square, 1)
     spread = jnp.where(same, jnp.broadcast_to(log_col, square), 0.0).sum(axis=1, keepdims=True)
     high, middle, low = three_parts(spread)
-    lane = lax.broadcasted_iota(jnp.int32, (words, wide - 256), 1) + 256
+    embed = embed_ref[...].astype(jnp.float32)
+    lane = lax.broadcasted_iota(jnp.int32, (words, WIDE - 256), 1) + 256
     tail = jnp.where(lane == depth, high, 0.0)
     tail = jnp.where(lane == depth + 1, middle, tail)
     tail = jnp.where(lane == depth + 2, low, tail)
     tail = jnp.where((lane >= depth + 3) & (lane < depth + 6), 1.0, tail)
-    embed = embed_ref[...].astype(jnp.float32)
-    padded = jnp.concatenate([embed, jnp.zeros((words, wide - depth), jnp.float32)], axis=1)
-    block = jnp.concatenate([padded[:, :256], padded[:, 256:] + tail], axis=1).astype(jnp.bfloat16)
+    padded = jnp.concatenate([embed, jnp.zeros((words, WIDE - depth), jnp.float32)], axis=1)
+    tail = tail + padded[:, 256:]
+    half_lane = lax.broadcasted_iota(jnp.int32, (8, TILE), 1)
+    last = jnp.where(half_lane < 64, tail[:8], pltpu.roll(tail[8:], 64, 1))
+    block = jnp.concatenate([padded[:, :128], padded[:, 128:256], last], axis=0).astype(jnp.bfloat16)
     for copy in range(copies):
         out_ref[copy] = block
+
+
+def unpack_words(packed):
+    blocks = packed.astype(jnp.float32)
+    last = blocks[:, 32:40, :]
+    lane = lax.broadcasted_iota(jnp.int32, last.shape, 2)
+    front = jnp.where(lane < 64, last, 0.0)
+    back = jnp.where(lane < 64, pltpu.roll(last, 64, 2), 0.0)
+    tail = jnp.concatenate([front, back], axis=1)
+    whole = jnp.concatenate([blocks[:, :16, :], blocks[:, 16:32, :], tail], axis=2)
+    return whole.astype(jnp.bfloat16)
 
 
 def prep_rows(embed_ref, marg_ref, total_ref, wide_ref, turned_ref):
@@ -65,14 +79,16 @@
     turned_ref[...] = whole.T.astype(jnp.bfloat16)
 
 
-def half_step(first, place, occ_ref, count_ref, wide_ref, turned_ref, own_ref, peer_ref, *rest):
+def half_step(first, occ_ref, count_ref, wide_ref, turned_ref, own_ref, peer_ref, *rest):
     if first:
         row_out, keep_ref, send_ref, turned_cols, residual_ref, held, arrived = rest
     else:
         row_in, row_out, keep_ref, send_ref, turned_cols, residual_ref, held, arrived = rest
-    which, core = place[0], place[1]
-    chips, words, wide = own_ref.shape
-    depth_rows = row_out.shape[0]
+    xl, core = lax.axis_index("xl"), lax.axis_index("core")
+    which = xl if first else 1 - xl
+    chips = own_ref.shape[0]
+    wide = wide_ref.shape[0]
+    depth_rows = 304
     rows, width = residual_ref.shape
     tiles = width // TILE
     blocks = rows // BLOCK
@@ -89,7 +105,7 @@
     for step in range(blocks):
         fetch(step).start()
 
-    own, peer = own_ref[...], peer_ref[...]
+    own, peer = unpack_words(own_ref[...]), unpack_words(peer_ref[...])
     low = jnp.where(core == 0, own, peer)
     high = jnp.where(core == 0, peer, own)
     pair = jnp.concatenate([low[:, None], high[:, None]], axis=1)
@@ -151,32 +167,28 @@
         send_ref[chip] = jnp.where(core == 0, packed[1], packed[0])
 
 
-def run_half(first, place, occ, count_view, wide_rows, turned_rows, own, peer, row_in):
+def run_half(first, occ, counted, wide_rows, turned_rows, own, peer, row_in):
     rows = turned_rows.shape[0]
-    chips, words, wide = own.shape
-    width = chips * 2 * words
-    depth_rows = 304
+    chips, wide = own.shape[0], wide_rows.shape[0]
+    width = chips * 32
+    blocks, tiles = rows // BLOCK, width // TILE
     smem = pl.BlockSpec(memory_space=pltpu.SMEM)
     vmem = pl.BlockSpec(memory_space=pltpu.VMEM)
-    operands = [place, occ, count_view, wide_rows, turned_rows, own, peer]
+    operands = [occ, counted, wide_rows, turned_rows, own, peer]
+    chunk = jax.ShapeDtypeStruct((chips, PACK, TILE), jnp.float32)
+    row_type = jnp.float32 if first else jnp.bfloat16
+    out_shape = [jax.ShapeDtypeStruct((304, rows), row_type), chunk, chunk]
+    scratch = [pltpu.VMEM((wide, width), jnp.bfloat16), pltpu.VMEM((rows, width), jnp.bfloat16)]
+    held = (blocks, BLOCK, tiles, TILE)
+    scratch += [pltpu.VMEM(held, jnp.int32), pltpu.SemaphoreType.DMA((blocks,))]
     if not first:
         operands.append(row_in)
-    chunk = jax.ShapeDtypeStruct((chips, PACK, TILE), jnp.float32)
     return pl.pallas_call(
         functools.partial(half_step, first),
-        in_specs=[smem, smem, pl.BlockSpec(memory_space=pltpu.HBM)] + [vmem] * (len(operands) - 3),
-        out_specs=[vmem] * 3,
-        scratch_shapes=[
-            pltpu.VMEM((wide, width), jnp.bfloat16),
-            pltpu.VMEM((rows, width), jnp.bfloat16),
-            pltpu.VMEM((rows // BLOCK, BLOCK, width // TILE, TILE), jnp.int32),
-            pltpu.SemaphoreType.DMA((rows // BLOCK,)),
-        ],
-        out_shape=[
-            jax.ShapeDtypeStruct((depth_rows, rows), jnp.float32 if first else jnp.bfloat16),
-            chunk,
-            chunk,
-        ],
+        in_specs=[smem, pl.BlockSpec(memory_space=pl.ANY)] + [vmem] * (len(operands) - 2),
+        out_specs=[vmem] * len(out_shape),
+        scratch_shapes=scratch,
+        out_shape=out_shape,
         compiler_params=pltpu.CompilerParams(vmem_limit_bytes=HALF_LIMIT),
         cost_estimate=pl.CostEstimate(
             flops=6 * rows * width * 300, bytes_accessed=8 * rows * width // 2,
@@ -185,9 +197,9 @@
     )(*operands)
 
 
-def join(place, keep_a, got_a, keep_b, got_b, out_ref):
+def join(keep_a, got_a, keep_b, got_b, out_ref):
     chips = keep_a.shape[0]
-    which = place[0]
+    which = lax.axis_index("xl")
     for at, keep, got in ((which, keep_a, got_a), (1 - which, keep_b, got_b)):
         for chip in range(chips):
             out_ref[at * chips + chip] = (keep[chip] + got[chip]).astype(jnp.bfloat16)
@@ -209,15 +221,13 @@
 
     depth, rows = row_embed.shape
     words = col_embed.shape[2]
-    core = lax.axis_index("core")
-    xl = lax.axis_index("xl")
     params = pltpu.CompilerParams(vmem_limit_bytes=VMEM_LIMIT)
     smem = pl.BlockSpec(memory_space=pltpu.SMEM)
     vmem = pl.BlockSpec(memory_space=pltpu.VMEM)
 
     fan_out = pl.pallas_call(
         prep_cols,
-        out_shape=jax.ShapeDtypeStruct((32, words, WIDE), jnp.bfloat16),
+        out_shape=jax.ShapeDtypeStruct((32, PACK, TILE), jnp.bfloat16),
         compiler_params=params,
     )(col_embed[:, 0, :].T, col_marg)
     quarter = lax.all_to_all(fan_out, ("y", "z"), 0, 0, tiled=True)
@@ -229,31 +239,34 @@
             jax.ShapeDtypeStruct((rows, WIDE), jnp.bfloat16),
         ],
         compiler_params=params,
-        cost_estimate=pl.CostEstimate(flops=rows * WIDE, bytes_accessed=4 * rows * WIDE, transcendentals=0),
+        cost_estimate=pl.CostEstimate(flops=rows * WIDE, bytes_accessed=40 * rows * WIDE, transcendentals=0),
     )(row_embed, row_marg[None, :], log_total)
+    quarter, wide_rows, turned_rows = lax.optimization_barrier(
+        (quarter, wide_rows, turned_rows)
+    )
     count_view = counts.reshape(rows, 16, TILE)
     occ = occupancy[:, 0, :]
 
     peer = lax.ppermute(quarter, "core", SWAP)
     far = lax.ppermute(quarter, "xl", SWAP)
+    row_part, keep_a, send_a = run_half(
+        True, occ, count_view, wide_rows, turned_rows, quarter, peer, None
+    )
+    far, row_part = lax.optimization_barrier((far, row_part))
     far_peer = lax.ppermute(far, "core", SWAP)
-    row_part, keep_a, send_a = run_half(
-        True, jnp.stack([xl, core]), occ, count_view, wide_rows, turned_rows, quarter, peer, None
-    )
     got_a = lax.ppermute(send_a, "core", SWAP)
     mine, keep_b, send_b = run_half(
-        False, jnp.stack([1 - xl, core]), occ, count_view, wide_rows, turned_rows, far, far_peer,
-        row_part,
+        False, occ, count_view, wide_rows, turned_rows, far, far_peer, row_part
     )
     got_b = lax.ppermute(send_b, "core", SWAP)
     theirs = lax.ppermute(mine, "xh", SWAP)
 
     outgoing = pl.pallas_call(
         join,
-        in_specs=[smem, vmem, vmem, vmem, vmem],
+        in_specs=[vmem] * 4,
         out_shape=jax.ShapeDtypeStruct((64, PACK, TILE), jnp.bfloat16),
         compiler_params=params,
-    )(xl[None], keep_a, got_a, keep_b, got_b)
+    )(keep_a, got_a, keep_b, got_b)
     arrived = lax.all_to_all(outgoing, ("xl", "y", "z"), 0, 0, tiled=True)
     grad_rows, grad_cols = pl.pallas_call(
         functools.partial(finish, 1.0 / math.sqrt(words * 256), 1.0 / math.sqrt(rows * 128)),

time: 89.3 us -> 82.9 us (0.928)
  blocking collectives: 23.5 us -> 0 us
  waiting for transfers between devices: 22.8 us -> 33.7 us
  starting transfers between devices: 22.1 us -> 27.3 us
  Pallas kernels: 16.9 us -> 17.9 us
    all_to_all x1 -> x0, blocking collectives: 23.5 us -> none  [body(): quarter = lax.all_to_all(fan_out, ('y', 'z'), 0, 0, tiled=True)]
    all_to_all x0 -> x1, starting transfers between devices: none -> 12 us  [body(): quarter = lax.all_to_all(fan_out, ('y', 'z'), 0, 0, tiled=True)]
    all_to_all x0 -> x1, waiting for transfers between devices: none -> 8.54 us  [body(): quarter = lax.all_to_all(fan_out, ('y', 'z'), 0, 0, tiled=True)]
    ppermute x1, starting transfers between devices: 4.63 us -> 0.78 us  [body(): far_peer = lax.ppermute(far, 'core', SWAP)]
    all_to_all x1, starting transfers between devices: 8.94 us -> 5.96 us  [body(): arrived = lax.all_to_all(outgoing, ('xl', 'y', 'z'), 0, 0, tiled=True)]
    ppermute x1, waiting for transfers between devices: 0.01 us -> 1.25 us  [body(): far_peer = lax.ppermute(far, 'core', SWAP)]
    pallas_call x4, Pallas kernels: 15.1 us -> 16.2 us  [the longest x2 14.3 us: run_half(): pl.pallas_call(functools.partial(half_step, first), in_specs=[smem, pl.Bl...]
    ppermute x1, waiting for transfers between devices: 0.01 us -> 1.05 us  [body(): far = lax.ppermute(quarter, 'xl', SWAP)]
  transfers between devices with their start and end apart: 7 -> 8, of which waited for: 2 -> 5; matrix products, arithmetic and copies ran while one was open for 0% -> 0% of each run, Pallas kernels for 16% -> 18%
where the time goes in v2:
time: 82.9 us; the launch traced here: 82.4 us
  waiting for transfers between devices  33.7 us (41%)
  starting transfers between devices  27.3 us (33%)
  Pallas kernels  17.9 us (22%)
  local copies, waits for them, and re-layouts  2.11 us (3%)
  between operations  1.37 us (2%)
    ppermute x1, waiting for transfers between devices, body(): theirs = lax.ppermute(mine, 'xh', SWAP)  21.1 us
    pallas_call x2, Pallas kernels, run_half(): pl.pallas_call(functools.partial(half_step, first), in_specs=[smem, pl.Bl...  14.3 us
    all_to_all x1, starting transfers between devices, body(): quarter = lax.all_to_all(fan_out, ('y', 'z'), 0, 0, tiled=True)  12 us
    all_to_all x1, waiting for transfers between devices, body(): quarter = lax.all_to_all(fan_out, ('y', 'z'), 0, 0, tiled=True)  8.54 us
    all_to_all x1, starting transfers between devices, body(): arrived = lax.all_to_all(outgoing, ('xl', 'y', 'z'), 0, 0, tiled=True)  5.96 us
    ppermute x1, starting transfers between devices, body(): peer = lax.ppermute(quarter, 'core', SWAP)  4.34 us
    ppermute x1, starting transfers between devices, body(): theirs = lax.ppermute(mine, 'xh', SWAP)  2.53 us
    unnamed x10, local copies, waits for them, and re-layouts  2.11 us
  transfers between devices with their start and end apart: 8, of which 5 were waited for; matrix products, arithmetic and copies ran while one was open for 0% of the time, Pallas kernels for 18%

profile of v2, /device:TPU:1, one launch (start us, length us, event | category | flops | bytes accessed | tf_op | source)
XLA Modules:
  0.0 82.4 jit_solution(6873917691832890506)
XLA Ops:
  0.6 0.0 copy-start
  0.6 0.0 copy-start.1
  0.7 0.0 copy-start.2
  0.7 0.8 copy-done.2
  1.4 0.0 copy-start.4
  1.4 0.7 copy-done.4
  2.1 0.9 %shard_map.86 = bf16[32,40,128]{2,1,0:T(8,128)(2,1)} custom-call(bf16[16,300]{1,0:T(8,128)(2,1)S(1)} %bitcast.11, s32[1,16]{1,0:T(1,128)S(1)} %copy-done.4), custom_call_target="tpu_custom_call" | custom-call | tf_op jit(solution)/shard_map/pallas_call | solution.py:228
  3.0 12.0 %all-to-all-start = ((bf16[32,40,128]{2,1,0:T(8,128)(2,1)}), bf16[32,40,128]{2,1,0:T(8,128)(2,1)S(1)}, u32[]{:S(2)}, u32[]{:S(2)}) async-start(bf16[32,40,128]{2,1,0:T(8,128)(2,1)} %shard_map.86), calls=%async_computation | async-start | bytes 655360 | tf_op jit(solution)/shard_map/all_to_all | solution.py:233
  15.7 0.0 copy-done
  15.7 0.0 copy-start.3
  15.7 0.7 copy-done.3
  16.4 0.3 shard_map.87
  16.6 8.5 %all-to-all-done.own_ref = bf16[32,40,128]{2,1,0:T(8,128)(2,1)S(1)} async-done(((bf16[32,40,128]{2,1,0:T(8,128)(2,1)}), bf16[32,40,128]{2,1,0:T(8,128)(2,1)S(1)}, u32[]{:S(2)}, u32[]{:S(2)}) %all-to-all-start) | async-done | bytes 327712 | tf_op jit(solution)/shard_map/all_to_all | solution.py:233
  25.2 4.3 %collective-permute-start.1 = (bf16[32,40,128]{2,1,0:T(8,128)(2,1)S(1)}, bf16[32,40,128]{2,1,0:T(8,128)(2,1)S(1)}, u32[]{:S(2)}, u32[]{:S(2)}) collective-permute-start(bf16[32,40,128]{2,1,0:T(8,128)(2,1)S(1)} %all-to-all-done.own_ref), channel_id=1, source_target_pairs={{0,2},{2,0},{1,3},{3,1},{4,6},{6,4},{5,7},{7,5},{8,10},{10,8},{9,1... | collective-permute-start | bytes 983048 | tf_op jit(solution)/shard_map/ppermute | solution.py:250
  29.5 1.2 %collective-permute-start = (bf16[32,40,128]{2,1,0:T(8,128)(2,1)S(1)}, bf16[32,40,128]{2,1,0:T(8,128)(2,1)S(1)}, u32[]{:S(2)}, u32[]{:S(2)}) collective-permute-start(bf16[32,40,128]{2,1,0:T(8,128)(2,1)S(1)} %all-to-all-done.own_ref), channel_id=1, source_target_pairs={{0,128},{128,0},{1,129},{129,1},{2,130},{130,2},{3,131},{131,3},{4... | collective-permute-start | bytes 983048 | tf_op jit(solution)/shard_map/ppermute | solution.py:251
  30.7 0.0 collective-permute-done.1.peer_ref
  30.8 0.0 copy-done.1
  30.8 7.0 %shard_map.88 = (f32[304,1024]{1,0:T(8,128)S(1)}, f32[32,40,128]{2,1,0:T(8,128)S(1)}, f32[32,40,128]{2,1,0:T(8,128)S(1)}) custom-call(s32[8,16]{1,0:T(8,128)S(1)} %bitcast.9, s32[1024,16,128]{2,1,0:T(8,128)} %bitcast.13, bf16[384,1024]{1,0:T(8,128)(2,1)S(1)} %get-tuple-element.19.wide_ref, bf16[1024,384]{1,0:T(8,128)(2,1)S(1)} %get-tuple-element.20.turned_ref, ...), custom_call_target="tpu_custom_call" | custom-call | flops 1887436800 | bytes 4194304 | tf_op jit(solution)/shard_map/pallas_call | solution.py:186
  37.8 1.0 %collective-permute-done.own_ref = bf16[32,40,128]{2,1,0:T(8,128)(2,1)S(1)} collective-permute-done((bf16[32,40,128]{2,1,0:T(8,128)(2,1)S(1)}, bf16[32,40,128]{2,1,0:T(8,128)(2,1)S(1)}, u32[]{:S(2)}, u32[]{:S(2)}) %collective-permute-start) | collective-permute-done | bytes 327712 | tf_op jit(solution)/shard_map/ppermute | solution.py:251
  38.9 0.8 collective-permute-start.2
  39.7 0.0 collective-permute-start.4
  39.7 1.3 %collective-permute-done.2.peer_ref = bf16[32,40,128]{2,1,0:T(8,128)(2,1)S(1)} collective-permute-done((bf16[32,40,128]{2,1,0:T(8,128)(2,1)S(1)}, bf16[32,40,128]{2,1,0:T(8,128)(2,1)S(1)}, u32[]{:S(2)}, u32[]{:S(2)}) %collective-permute-start.2) | collective-permute-done | bytes 327712 | tf_op jit(solution)/shard_map/ppermute | solution.py:256
  40.9 7.3 %shard_map.89 = (bf16[304,1024]{1,0:T(8,128)(2,1)S(1)}, f32[32,40,128]{2,1,0:T(8,128)S(1)}, f32[32,40,128]{2,1,0:T(8,128)S(1)}) custom-call(s32[8,16]{1,0:T(8,128)S(1)} %bitcast.10, s32[1024,16,128]{2,1,0:T(8,128)} %bitcast.14, bf16[384,1024]{1,0:T(8,128)(2,1)S(1)} %get-tuple-element.19.wide_ref, bf16[1024,384]{1,0:T(8,128)(2,1)S(1)} %get-tuple-element.20.turned_ref, ...), custom_call_target="tpu_custom_call" | custom-call | flops 1887436800 | bytes 4194304 | tf_op jit(solution)/shard_map/pallas_call | solution.py:186
  48.2 0.5 collective-permute-start.5
  48.7 0.0 collective-permute-done.4.got_a
  48.7 1.7 %collective-permute-done.5.got_b = f32[32,40,128]{2,1,0:T(8,128)S(1)} collective-permute-done((f32[32,40,128]{2,1,0:T(8,128)S(1)}, f32[32,40,128]{2,1,0:T(8,128)S(1)}, u32[]{:S(2)}, u32[]{:S(2)}) %collective-permute-start.5) | collective-permute-done | bytes 655392 | tf_op jit(solution)/shard_map/ppermute | solution.py:261
  50.4 1.0 %shard_map.90 = bf16[64,40,128]{2,1,0:T(8,128)(2,1)} custom-call(f32[32,40,128]{2,1,0:T(8,128)S(1)} %get-tuple-element.26.keep_a, f32[32,40,128]{2,1,0:T(8,128)S(1)} %collective-permute-done.4.got_a, f32[32,40,128]{2,1,0:T(8,128)S(1)} %get-tuple-element.28.keep_b, f32[32,40,128]{2,1,0:T(8,128)S(1)} %collective-permute-done.5.got_b), custom_call_target="tpu_custom_call" | custom-call | tf_op jit(solution)/shard_map/pallas_call | solution.py:264
  51.3 6.0 %all-to-all-start.1 = ((bf16[64,40,128]{2,1,0:T(8,128)(2,1)}), bf16[64,40,128]{2,1,0:T(8,128)(2,1)S(1)}, u32[]{:S(2)}, u32[]{:S(2)}) async-start(bf16[64,40,128]{2,1,0:T(8,128)(2,1)} %shard_map.90), calls=%async_computation.1 | async-start | bytes 1310720 | tf_op jit(solution)/shard_map/all_to_all | solution.py:270
  57.3 2.5 %collective-permute-start.3 = (bf16[304,1024]{1,0:T(8,128)(2,1)S(1)}, bf16[304,1024]{1,0:T(8,128)(2,1)S(1)}, u32[]{:S(2)}, u32[]{:S(2)}) collective-permute-start(bf16[304,1024]{1,0:T(8,128)(2,1)S(1)} %get-tuple-element.25.mine_ref), channel_id=1, source_target_pairs={{0,1},{1,0},{2,3},{3,2},{4,5},{5,4},{6,7},{7,6},{8,9},{9,8},{10,11... | collective-permute-start | bytes 1867784 | tf_op jit(solution)/shard_map/ppermute | solution.py:262
  59.9 21.1 %collective-permute-done.3.theirs_ref = bf16[304,1024]{1,0:T(8,128)(2,1)S(1)} collective-permute-done((bf16[304,1024]{1,0:T(8,128)(2,1)S(1)}, bf16[304,1024]{1,0:T(8,128)(2,1)S(1)}, u32[]{:S(2)}, u32[]{:S(2)}) %collective-permute-start.3) | collective-permute-done | bytes 622624 | tf_op jit(solution)/shard_map/ppermute | solution.py:262
  81.0 0.0 all-to-all-done.1.got_ref
  81.0 1.5 %shard_map.91 = (f32[300,1024]{1,0:T(8,128)}, f32[16,300]{1,0:T(8,128)}) custom-call(bf16[304,1024]{1,0:T(8,128)(2,1)S(1)} %get-tuple-element.25.mine_ref, bf16[304,1024]{1,0:T(8,128)(2,1)S(1)} %collective-permute-done.3.theirs_ref, bf16[64,40,128]{2,1,0:T(8,128)(2,1)S(1)} %all-to-all-done.1.got_ref), custom_call_target="tpu_custom_call" | custom-call | tf_op jit(solution)/shard_map/pallas_call | solution.py:271
Async XLA Ops:
  0.6 15.0 %copy-start = (bf16[300,1024]{1,0:T(8,128)(2,1)S(1)}, bf16[300,1024]{1,0:T(8,128)(2,1)}, u32[]{:S(2)}) copy-start(bf16[300,1024]{1,0:T(8,128)(2,1)} %embed_ref.1) | copy-start | bytes 1843204
  0.6 30.2 %copy-start.1 = (s32[8,1,16]{2,1,0:T(1,128)S(1)}, s32[8,1,16]{2,1,0:T(1,128)}, u32[]{:S(2)}) copy-start(s32[8,1,16]{2,1,0:T(1,128)} %param.10) | copy-start | bytes 1540
  0.7 0.8 copy-start.2
  1.4 0.7 copy-start.4
  3.0 22.2 %all-to-all-start = ((bf16[32,40,128]{2,1,0:T(8,128)(2,1)}), bf16[32,40,128]{2,1,0:T(8,128)(2,1)S(1)}, u32[]{:S(2)}, u32[]{:S(2)}) async-start(bf16[32,40,128]{2,1,0:T(8,128)(2,1)} %shard_map.86), calls=%async_computation | async-start | bytes 655360 | tf_op jit(solution)/shard_map/all_to_all | solution.py:233
  15.7 0.7 copy-start.3
  25.2 5.6 %collective-permute-start.1 = (bf16[32,40,128]{2,1,0:T(8,128)(2,1)S(1)}, bf16[32,40,128]{2,1,0:T(8,128)(2,1)S(1)}, u32[]{:S(2)}, u32[]{:S(2)}) collective-permute-start(bf16[32,40,128]{2,1,0:T(8,128)(2,1)S(1)} %all-to-all-done.own_ref), channel_id=1, source_target_pairs={{0,2},{2,0},{1,3},{3,1},{4,6},{6,4},{5,7},{7,5},{8,10},{10,8},{9,1... | collective-permute-start | bytes 983048 | tf_op jit(solution)/shard_map/ppermute | solution.py:250
  29.5 9.3 %collective-permute-start = (bf16[32,40,128]{2,1,0:T(8,128)(2,1)S(1)}, bf16[32,40,128]{2,1,0:T(8,128)(2,1)S(1)}, u32[]{:S(2)}, u32[]{:S(2)}) collective-permute-start(bf16[32,40,128]{2,1,0:T(8,128)(2,1)S(1)} %all-to-all-done.own_ref), channel_id=1, source_target_pairs={{0,128},{128,0},{1,129},{129,1},{2,130},{130,2},{3,131},{131,3},{4... | collective-permute-start | bytes 983048 | tf_op jit(solution)/shard_map/ppermute | solution.py:251
  38.9 2.0 %collective-permute-start.2 = (bf16[32,40,128]{2,1,0:T(8,128)(2,1)S(1)}, bf16[32,40,128]{2,1,0:T(8,128)(2,1)S(1)}, u32[]{:S(2)}, u32[]{:S(2)}) collective-permute-start(bf16[32,40,128]{2,1,0:T(8,128)(2,1)S(1)} %collective-permute-done.own_ref), channel_id=1, source_target_pairs={{0,2},{2,0},{1,3},{3,1},{4,6},{6,4},{5,7},{7,5},{8,10},{10,8},{9,1... | collective-permute-start | bytes 983048 | tf_op jit(solution)/shard_map/ppermute | solution.py:256
  39.7 9.0 %collective-permute-start.4 = (f32[32,40,128]{2,1,0:T(8,128)S(1)}, f32[32,40,128]{2,1,0:T(8,128)S(1)}, u32[]{:S(2)}, u32[]{:S(2)}) collective-permute-start(f32[32,40,128]{2,1,0:T(8,128)S(1)} %get-tuple-element.27), channel_id=1, source_target_pairs={{0,2},{2,0},{1,3},{3,1},{4,6},{6,4},{5,7},{7,5},{8,10},{10,8},{9,1... | collective-permute-start | bytes 1966088 | tf_op jit(solution)/shard_map/ppermute | solution.py:257
  48.2 2.2 %collective-permute-start.5 = (f32[32,40,128]{2,1,0:T(8,128)S(1)}, f32[32,40,128]{2,1,0:T(8,128)S(1)}, u32[]{:S(2)}, u32[]{:S(2)}) collective-permute-start(f32[32,40,128]{2,1,0:T(8,128)S(1)} %get-tuple-element.29), channel_id=1, source_target_pairs={{0,2},{2,0},{1,3},{3,1},{4,6},{6,4},{5,7},{7,5},{8,10},{10,8},{9,1... | collective-permute-start | bytes 1966088 | tf_op jit(solution)/shard_map/ppermute | solution.py:261
  51.3 29.6 %all-to-all-start.1 = ((bf16[64,40,128]{2,1,0:T(8,128)(2,1)}), bf16[64,40,128]{2,1,0:T(8,128)(2,1)S(1)}, u32[]{:S(2)}, u32[]{:S(2)}) async-start(bf16[64,40,128]{2,1,0:T(8,128)(2,1)} %shard_map.90), calls=%async_computation.1 | async-start | bytes 1310720 | tf_op jit(solution)/shard_map/all_to_all | solution.py:270
  57.3 23.6 %collective-permute-start.3 = (bf16[304,1024]{1,0:T(8,128)(2,1)S(1)}, bf16[304,1024]{1,0:T(8,128)(2,1)S(1)}, u32[]{:S(2)}, u32[]{:S(2)}) collective-permute-start(bf16[304,1024]{1,0:T(8,128)(2,1)S(1)} %get-tuple-element.25.mine_ref), channel_id=1, source_target_pairs={{0,1},{1,0},{2,3},{3,2},{4,5},{5,4},{6,7},{7,6},{8,9},{9,8},{10,11... | collective-permute-start | bytes 1867784 | tf_op jit(solution)/shard_map/ppermute | solution.py:262

commit v3 on v2

--- a/solution.py
+++ b/solution.py
@@ -15,6 +15,7 @@
 WIDE = 384
 BLOCK = 256
 PACK = 40
+FINISH_FLOPS = 100_000_000_000
 VMEM_LIMIT = 24 * 1024 * 1024
 HALF_LIMIT = 48 * 1024 * 1024
 SWAP = [(0, 1), (1, 0)]
@@ -110,7 +111,7 @@
     high = jnp.where(core == 0, peer, own)
     pair = jnp.concatenate([low[:, None], high[:, None]], axis=1)
     turned_cols[...] = pair.reshape(width, wide).T
-    @pl.loop(0, blocks)
+    @pl.loop(0, blocks, unroll=True)
     def _(step):
         fetch(step).wait()
         count_flat = held.at[step].reshape(BLOCK * tiles, TILE)
@@ -205,15 +206,18 @@
             out_ref[at * chips + chip] = (keep[chip] + got[chip]).astype(jnp.bfloat16)
 
 
-def finish(row_scale, col_scale, mine_ref, theirs_ref, got_ref, rows_ref, cols_ref):
-    depth = rows_ref.shape[0]
+def finish_rows(scale, mine_ref, theirs_ref, out_ref):
     both = mine_ref[...].astype(jnp.float32) + theirs_ref[...].astype(jnp.float32)
-    rows_ref[...] = both[:depth] * row_scale
-    total = got_ref[...].astype(jnp.float32).sum(axis=0) * col_scale
+    out_ref[...] = both[: out_ref.shape[0]] * scale
+
+
+def finish_cols(scale, got_ref, out_ref):
+    depth = out_ref.shape[1]
+    total = got_ref[...].astype(jnp.float32).sum(axis=0) * scale
     last = total[32:40]
     turned = pltpu.roll(last, 64, 1)
-    cols_ref[0:8, :] = jnp.concatenate([total[0:8], total[16:24], last], axis=1)[:, :depth]
-    cols_ref[8:16, :] = jnp.concatenate([total[8:16], total[24:32], turned], axis=1)[:, :depth]
+    out_ref[0:8, :] = jnp.concatenate([total[0:8], total[16:24], last], axis=1)[:, :depth]
+    out_ref[8:16, :] = jnp.concatenate([total[8:16], total[24:32], turned], axis=1)[:, :depth]
 
 
 def body(row_embed, col_embed, counts, occupancy, row_marg, col_marg, log_total):
@@ -268,16 +272,19 @@
         compiler_params=params,
     )(keep_a, got_a, keep_b, got_b)
     arrived = lax.all_to_all(outgoing, ("xl", "y", "z"), 0, 0, tiled=True)
-    grad_rows, grad_cols = pl.pallas_call(
-        functools.partial(finish, 1.0 / math.sqrt(words * 256), 1.0 / math.sqrt(rows * 128)),
-        in_specs=[vmem, vmem, vmem],
-        out_specs=[vmem, vmem],
-        out_shape=[
-            jax.ShapeDtypeStruct((depth, rows), jnp.float32),
-            jax.ShapeDtypeStruct((words, depth), jnp.float32),
-        ],
-        compiler_params=params,
-    )(mine, theirs, arrived)
+    grad_rows = pl.pallas_call(
+        functools.partial(finish_rows, 1.0 / math.sqrt(words * 256)),
+        out_shape=jax.ShapeDtypeStruct((depth, rows), jnp.float32),
+        compiler_params=params,
+        cost_estimate=pl.CostEstimate(
+            flops=FINISH_FLOPS, bytes_accessed=4 * depth * rows * 2, transcendentals=0
+        ),
+    )(mine, theirs)
+    grad_cols = pl.pallas_call(
+        functools.partial(finish_cols, 1.0 / math.sqrt(rows * 128)),
+        out_shape=jax.ShapeDtypeStruct((words, depth), jnp.float32),
+        compiler_params=params,
+    )(arrived)
     return (grad_rows, grad_cols.T[:, None, :])
 
 

time: 82.9 us -> 79.1 us (0.954); the launches traced: 82.4 us -> 77.5 us
  waiting for transfers between devices: 33.7 us -> 30.2 us
    ppermute x1, waiting for transfers between devices: 21.1 us -> 10.2 us  [body(): theirs = lax.ppermute(mine, 'xh', SWAP)]
    all_to_all x1, waiting for transfers between devices: 0.01 us -> 8.57 us  [body(): arrived = lax.all_to_all(outgoing, ('xl', 'y', 'z'), 0, 0, tiled=True)]
    ppermute x1, waiting for transfers between devices: 1.72 us -> 0.01 us  [body(): got_b = lax.ppermute(send_b, 'core', SWAP)]
    pallas_call x2, Pallas kernels: 14.3 us -> 13.1 us  [run_half(): pl.pallas_call(functools.partial(half_step, first), in_specs=[smem, pl.Bl...]
    all_to_all x1, starting transfers between devices: 5.96 us -> 5.06 us  [body(): arrived = lax.all_to_all(outgoing, ('xl', 'y', 'z'), 0, 0, tiled=True)]
    pallas_call x1 -> x2, Pallas kernels: 1.46 us -> 1.97 us  [the longest x1 1.2 us: body(): pl.pallas_call(functools.partial(finish_rows, 1.0 / math.sqrt(words * 256...]
  transfers between devices with their start and end apart: 8 -> 8, of which waited for: 5 -> 5; matrix products, arithmetic and copies ran while one was open for 0% -> 0% of each run, Pallas kernels for 18% -> 20%
where the time goes in v3:
time: 79.1 us; the launch traced here: 77.5 us
  waiting for transfers between devices  30.2 us (38%)
  starting transfers between devices  26.6 us (34%)
  Pallas kernels  17.2 us (22%)
  local copies, waits for them, and re-layouts  2.11 us (3%)
  between operations  1.37 us (2%)
    pallas_call x2, Pallas kernels, run_half(): pl.pallas_call(functools.partial(half_step, first), in_specs=[smem, pl.Bl...  13.1 us
    all_to_all x1, starting transfers between devices, body(): quarter = lax.all_to_all(fan_out, ('y', 'z'), 0, 0, tiled=True)  12 us
    ppermute x1, waiting for transfers between devices, body(): theirs = lax.ppermute(mine, 'xh', SWAP)  10.2 us
    all_to_all x1, waiting for transfers between devices, body(): arrived = lax.all_to_all(outgoing, ('xl', 'y', 'z'), 0, 0, tiled=True)  8.57 us
    all_to_all x1, waiting for transfers between devices, body(): quarter = lax.all_to_all(fan_out, ('y', 'z'), 0, 0, tiled=True)  8.54 us
    all_to_all x1, starting transfers between devices, body(): arrived = lax.all_to_all(outgoing, ('xl', 'y', 'z'), 0, 0, tiled=True)  5.06 us
    ppermute x1, starting transfers between devices, body(): peer = lax.ppermute(quarter, 'core', SWAP)  4.34 us
    ppermute x1, starting transfers between devices, body(): theirs = lax.ppermute(mine, 'xh', SWAP)  2.75 us
  transfers between devices with their start and end apart: 8, of which 5 were waited for; matrix products, arithmetic and copies ran while one was open for 0% of the time, Pallas kernels for 20%

profile of v3, /device:TPU:1, one launch (start us, length us, event | category | flops | bytes accessed | tf_op | source)
XLA Modules:
  0.0 77.5 jit_solution(7794705190886263032)
XLA Ops:
  0.6 0.0 copy-start
  0.6 0.0 copy-start.1
  0.7 0.0 copy-start.2
  0.7 0.8 copy-done.2
  1.4 0.0 copy-start.4
  1.4 0.7 copy-done.4
  2.1 0.9 %shard_map.86 = bf16[32,40,128]{2,1,0:T(8,128)(2,1)} custom-call(bf16[16,300]{1,0:T(8,128)(2,1)S(1)} %bitcast.11, s32[1,16]{1,0:T(1,128)S(1)} %copy-done.4), custom_call_target="tpu_custom_call" | custom-call | tf_op jit(solution)/shard_map/pallas_call | solution.py:232
  3.0 12.0 %all-to-all-start = ((bf16[32,40,128]{2,1,0:T(8,128)(2,1)}), bf16[32,40,128]{2,1,0:T(8,128)(2,1)S(1)}, u32[]{:S(2)}, u32[]{:S(2)}) async-start(bf16[32,40,128]{2,1,0:T(8,128)(2,1)} %shard_map.86), calls=%async_computation | async-start | bytes 655360 | tf_op jit(solution)/shard_map/all_to_all | solution.py:237
  15.7 0.0 copy-done
  15.7 0.0 copy-start.3
  15.7 0.7 copy-done.3
  16.4 0.3 shard_map.87
  16.6 8.5 %all-to-all-done.own_ref = bf16[32,40,128]{2,1,0:T(8,128)(2,1)S(1)} async-done(((bf16[32,40,128]{2,1,0:T(8,128)(2,1)}), bf16[32,40,128]{2,1,0:T(8,128)(2,1)S(1)}, u32[]{:S(2)}, u32[]{:S(2)}) %all-to-all-start) | async-done | bytes 327712 | tf_op jit(solution)/shard_map/all_to_all | solution.py:237
  25.2 4.3 %collective-permute-start.1 = (bf16[32,40,128]{2,1,0:T(8,128)(2,1)S(1)}, bf16[32,40,128]{2,1,0:T(8,128)(2,1)S(1)}, u32[]{:S(2)}, u32[]{:S(2)}) collective-permute-start(bf16[32,40,128]{2,1,0:T(8,128)(2,1)S(1)} %all-to-all-done.own_ref), channel_id=1, source_target_pairs={{0,2},{2,0},{1,3},{3,1},{4,6},{6,4},{5,7},{7,5},{8,10},{10,8},{9,1... | collective-permute-start | bytes 983048 | tf_op jit(solution)/shard_map/ppermute | solution.py:254
  29.5 1.2 %collective-permute-start = (bf16[32,40,128]{2,1,0:T(8,128)(2,1)S(1)}, bf16[32,40,128]{2,1,0:T(8,128)(2,1)S(1)}, u32[]{:S(2)}, u32[]{:S(2)}) collective-permute-start(bf16[32,40,128]{2,1,0:T(8,128)(2,1)S(1)} %all-to-all-done.own_ref), channel_id=1, source_target_pairs={{0,128},{128,0},{1,129},{129,1},{2,130},{130,2},{3,131},{131,3},{4... | collective-permute-start | bytes 983048 | tf_op jit(solution)/shard_map/ppermute | solution.py:255
  30.7 0.0 collective-permute-done.1.peer_ref
  30.8 0.0 copy-done.1
  30.8 6.5 %shard_map.88 = (f32[304,1024]{1,0:T(8,128)S(1)}, f32[32,40,128]{2,1,0:T(8,128)S(1)}, f32[32,40,128]{2,1,0:T(8,128)S(1)}) custom-call(s32[8,16]{1,0:T(8,128)S(1)} %bitcast.9, s32[1024,16,128]{2,1,0:T(8,128)} %bitcast.13, bf16[384,1024]{1,0:T(8,128)(2,1)S(1)} %get-tuple-element.17.wide_ref, bf16[1024,384]{1,0:T(8,128)(2,1)S(1)} %get-tuple-element.18.turned_ref, ...), custom_call_target="tpu_custom_call" | custom-call | flops 1887436800 | bytes 4194304 | tf_op jit(solution)/shard_map/pallas_call | solution.py:187
  37.3 1.6 %collective-permute-done.own_ref = bf16[32,40,128]{2,1,0:T(8,128)(2,1)S(1)} collective-permute-done((bf16[32,40,128]{2,1,0:T(8,128)(2,1)S(1)}, bf16[32,40,128]{2,1,0:T(8,128)(2,1)S(1)}, u32[]{:S(2)}, u32[]{:S(2)}) %collective-permute-start) | collective-permute-done | bytes 327712 | tf_op jit(solution)/shard_map/ppermute | solution.py:255
  38.9 0.8 %collective-permute-start.2 = (bf16[32,40,128]{2,1,0:T(8,128)(2,1)S(1)}, bf16[32,40,128]{2,1,0:T(8,128)(2,1)S(1)}, u32[]{:S(2)}, u32[]{:S(2)}) collective-permute-start(bf16[32,40,128]{2,1,0:T(8,128)(2,1)S(1)} %collective-permute-done.own_ref), channel_id=1, source_target_pairs={{0,2},{2,0},{1,3},{3,1},{4,6},{6,4},{5,7},{7,5},{8,10},{10,8},{9,1... | collective-permute-start | bytes 983048 | tf_op jit(solution)/shard_map/ppermute | solution.py:260
  39.7 0.0 collective-permute-start.4
  39.7 1.3 %collective-permute-done.2.peer_ref = bf16[32,40,128]{2,1,0:T(8,128)(2,1)S(1)} collective-permute-done((bf16[32,40,128]{2,1,0:T(8,128)(2,1)S(1)}, bf16[32,40,128]{2,1,0:T(8,128)(2,1)S(1)}, u32[]{:S(2)}, u32[]{:S(2)}) %collective-permute-start.2) | collective-permute-done | bytes 327712 | tf_op jit(solution)/shard_map/ppermute | solution.py:260
  40.9 6.6 %shard_map.89 = (bf16[304,1024]{1,0:T(8,128)(2,1)S(1)}, f32[32,40,128]{2,1,0:T(8,128)S(1)}, f32[32,40,128]{2,1,0:T(8,128)S(1)}) custom-call(s32[8,16]{1,0:T(8,128)S(1)} %bitcast.10, s32[1024,16,128]{2,1,0:T(8,128)} %bitcast.14, bf16[384,1024]{1,0:T(8,128)(2,1)S(1)} %get-tuple-element.17.wide_ref, bf16[1024,384]{1,0:T(8,128)(2,1)S(1)} %get-tuple-element.18.turned_ref, ...), custom_call_target="tpu_custom_call" | custom-call | flops 1887436800 | bytes 4194304 | tf_op jit(solution)/shard_map/pallas_call | solution.py:187
  47.5 0.5 collective-permute-start.5
  48.0 2.7 %collective-permute-start.3 = (bf16[304,1024]{1,0:T(8,128)(2,1)S(1)}, bf16[304,1024]{1,0:T(8,128)(2,1)S(1)}, u32[]{:S(2)}, u32[]{:S(2)}) collective-permute-start(bf16[304,1024]{1,0:T(8,128)(2,1)S(1)} %get-tuple-element.23.mine_ref), channel_id=1, source_target_pairs={{0,1},{1,0},{2,3},{3,2},{4,5},{5,4},{6,7},{7,6},{8,9},{9,8},{10,11... | collective-permute-start | bytes 1867784 | tf_op jit(solution)/shard_map/ppermute | solution.py:266
  50.7 0.0 collective-permute-done.4.got_a
  50.7 0.0 collective-permute-done.5.got_b
  50.7 1.0 %shard_map.91 = bf16[64,40,128]{2,1,0:T(8,128)(2,1)} custom-call(f32[32,40,128]{2,1,0:T(8,128)S(1)} %get-tuple-element.24.keep_a, f32[32,40,128]{2,1,0:T(8,128)S(1)} %collective-permute-done.4.got_a, f32[32,40,128]{2,1,0:T(8,128)S(1)} %get-tuple-element.26.keep_b, f32[32,40,128]{2,1,0:T(8,128)S(1)} %collective-permute-done.5.got_b), custom_call_target="tpu_custom_call" | custom-call | tf_op jit(solution)/shard_map/pallas_call | solution.py:268
  51.7 5.1 %all-to-all-start.1 = ((bf16[64,40,128]{2,1,0:T(8,128)(2,1)}), bf16[64,40,128]{2,1,0:T(8,128)(2,1)S(1)}, u32[]{:S(2)}, u32[]{:S(2)}) async-start(bf16[64,40,128]{2,1,0:T(8,128)(2,1)} %shard_map.91), calls=%async_computation.1 | async-start | bytes 1310720 | tf_op jit(solution)/shard_map/all_to_all | solution.py:274
  56.8 10.2 %collective-permute-done.3.theirs_ref = bf16[304,1024]{1,0:T(8,128)(2,1)S(1)} collective-permute-done((bf16[304,1024]{1,0:T(8,128)(2,1)S(1)}, bf16[304,1024]{1,0:T(8,128)(2,1)S(1)}, u32[]{:S(2)}, u32[]{:S(2)}) %collective-permute-start.3) | collective-permute-done | bytes 622624 | tf_op jit(solution)/shard_map/ppermute | solution.py:266
  67.0 1.2 %shard_map.90 = f32[300,1024]{1,0:T(8,128)} custom-call(bf16[304,1024]{1,0:T(8,128)(2,1)S(1)} %get-tuple-element.23.mine_ref, bf16[304,1024]{1,0:T(8,128)(2,1)S(1)} %collective-permute-done.3.theirs_ref), custom_call_target="tpu_custom_call" | custom-call | flops 99999997952 | bytes 2457600 | tf_op jit(solution)/shard_map/pallas_call | solution.py:275
  68.2 8.6 %all-to-all-done.1.got_ref = bf16[64,40,128]{2,1,0:T(8,128)(2,1)S(1)} async-done(((bf16[64,40,128]{2,1,0:T(8,128)(2,1)}), bf16[64,40,128]{2,1,0:T(8,128)(2,1)S(1)}, u32[]{:S(2)}, u32[]{:S(2)}) %all-to-all-start.1) | async-done | bytes 655392 | tf_op jit(solution)/shard_map/all_to_all | solution.py:274
  76.8 0.8 %shard_map.92 = f32[16,300]{1,0:T(8,128)} custom-call(bf16[64,40,128]{2,1,0:T(8,128)(2,1)S(1)} %all-to-all-done.1.got_ref), custom_call_target="tpu_custom_call" | custom-call | tf_op jit(solution)/shard_map/pallas_call | solution.py:283
Async XLA Ops:
  0.6 15.0 %copy-start = (bf16[300,1024]{1,0:T(8,128)(2,1)S(1)}, bf16[300,1024]{1,0:T(8,128)(2,1)}, u32[]{:S(2)}) copy-start(bf16[300,1024]{1,0:T(8,128)(2,1)} %embed_ref.1) | copy-start | bytes 1843204
  0.6 30.2 %copy-start.1 = (s32[8,1,16]{2,1,0:T(1,128)S(1)}, s32[8,1,16]{2,1,0:T(1,128)}, u32[]{:S(2)}) copy-start(s32[8,1,16]{2,1,0:T(1,128)} %param.10) | copy-start | bytes 1540
  0.7 0.8 copy-start.2
  1.4 0.7 copy-start.4
  3.0 22.2 %all-to-all-start = ((bf16[32,40,128]{2,1,0:T(8,128)(2,1)}), bf16[32,40,128]{2,1,0:T(8,128)(2,1)S(1)}, u32[]{:S(2)}, u32[]{:S(2)}) async-start(bf16[32,40,128]{2,1,0:T(8,128)(2,1)} %shard_map.86), calls=%async_computation | async-start | bytes 655360 | tf_op jit(solution)/shard_map/all_to_all | solution.py:237
  15.7 0.7 copy-start.3
  25.2 5.6 %collective-permute-start.1 = (bf16[32,40,128]{2,1,0:T(8,128)(2,1)S(1)}, bf16[32,40,128]{2,1,0:T(8,128)(2,1)S(1)}, u32[]{:S(2)}, u32[]{:S(2)}) collective-permute-start(bf16[32,40,128]{2,1,0:T(8,128)(2,1)S(1)} %all-to-all-done.own_ref), channel_id=1, source_target_pairs={{0,2},{2,0},{1,3},{3,1},{4,6},{6,4},{5,7},{7,5},{8,10},{10,8},{9,1... | collective-permute-start | bytes 983048 | tf_op jit(solution)/shard_map/ppermute | solution.py:254
  29.5 9.3 %collective-permute-start = (bf16[32,40,128]{2,1,0:T(8,128)(2,1)S(1)}, bf16[32,40,128]{2,1,0:T(8,128)(2,1)S(1)}, u32[]{:S(2)}, u32[]{:S(2)}) collective-permute-start(bf16[32,40,128]{2,1,0:T(8,128)(2,1)S(1)} %all-to-all-done.own_ref), channel_id=1, source_target_pairs={{0,128},{128,0},{1,129},{129,1},{2,130},{130,2},{3,131},{131,3},{4... | collective-permute-start | bytes 983048 | tf_op jit(solution)/shard_map/ppermute | solution.py:255
  38.9 2.0 %collective-permute-start.2 = (bf16[32,40,128]{2,1,0:T(8,128)(2,1)S(1)}, bf16[32,40,128]{2,1,0:T(8,128)(2,1)S(1)}, u32[]{:S(2)}, u32[]{:S(2)}) collective-permute-start(bf16[32,40,128]{2,1,0:T(8,128)(2,1)S(1)} %collective-permute-done.own_ref), channel_id=1, source_target_pairs={{0,2},{2,0},{1,3},{3,1},{4,6},{6,4},{5,7},{7,5},{8,10},{10,8},{9,1... | collective-permute-start | bytes 983048 | tf_op jit(solution)/shard_map/ppermute | solution.py:260
  39.7 11.1 %collective-permute-start.4 = (f32[32,40,128]{2,1,0:T(8,128)S(1)}, f32[32,40,128]{2,1,0:T(8,128)S(1)}, u32[]{:S(2)}, u32[]{:S(2)}) collective-permute-start(f32[32,40,128]{2,1,0:T(8,128)S(1)} %get-tuple-element.25), channel_id=1, source_target_pairs={{0,2},{2,0},{1,3},{3,1},{4,6},{6,4},{5,7},{7,5},{8,10},{10,8},{9,1... | collective-permute-start | bytes 1966088 | tf_op jit(solution)/shard_map/ppermute | solution.py:261
  47.5 3.2 %collective-permute-start.5 = (f32[32,40,128]{2,1,0:T(8,128)S(1)}, f32[32,40,128]{2,1,0:T(8,128)S(1)}, u32[]{:S(2)}, u32[]{:S(2)}) collective-permute-start(f32[32,40,128]{2,1,0:T(8,128)S(1)} %get-tuple-element.27), channel_id=1, source_target_pairs={{0,2},{2,0},{1,3},{3,1},{4,6},{6,4},{5,7},{7,5},{8,10},{10,8},{9,1... | collective-permute-start | bytes 1966088 | tf_op jit(solution)/shard_map/ppermute | solution.py:265
  48.0 19.0 %collective-permute-start.3 = (bf16[304,1024]{1,0:T(8,128)(2,1)S(1)}, bf16[304,1024]{1,0:T(8,128)(2,1)S(1)}, u32[]{:S(2)}, u32[]{:S(2)}) collective-permute-start(bf16[304,1024]{1,0:T(8,128)(2,1)S(1)} %get-tuple-element.23.mine_ref), channel_id=1, source_target_pairs={{0,1},{1,0},{2,3},{3,2},{4,5},{5,4},{6,7},{7,6},{8,9},{9,8},{10,11... | collective-permute-start | bytes 1867784 | tf_op jit(solution)/shard_map/ppermute | solution.py:266
  51.7 25.1 %all-to-all-start.1 = ((bf16[64,40,128]{2,1,0:T(8,128)(2,1)}), bf16[64,40,128]{2,1,0:T(8,128)(2,1)S(1)}, u32[]{:S(2)}, u32[]{:S(2)}) async-start(bf16[64,40,128]{2,1,0:T(8,128)(2,1)} %shard_map.91), calls=%async_computation.1 | async-start | bytes 1310720 | tf_op jit(solution)/shard_map/all_to_all | solution.py:274

commit v4 on v3

--- a/solution.py
+++ b/solution.py
@@ -198,12 +198,19 @@
     )(*operands)
 
 
-def join(keep_a, got_a, keep_b, got_b, out_ref):
-    chips = keep_a.shape[0]
-    which = lax.axis_index("xl")
-    for at, keep, got in ((which, keep_a, got_a), (1 - which, keep_b, got_b)):
-        for chip in range(chips):
-            out_ref[at * chips + chip] = (keep[chip] + got[chip]).astype(jnp.bfloat16)
+def join_near(keep, got, out_ref):
+    chips = keep.shape[0]
+    for chip in range(chips):
+        out_ref[chip] = (keep[chip] + got[chip]).astype(jnp.bfloat16)
+
+
+def join_far(keep, got, near_ref, out_ref):
+    chips = keep.shape[0]
+    for chip in range(chips):
+        out_ref[lax.axis_index("xl") * chips + chip] = near_ref[chip]
+        out_ref[(1 - lax.axis_index("xl")) * chips + chip] = (keep[chip] + got[chip]).astype(
+            jnp.bfloat16
+        )
 
 
 def finish_rows(scale, mine_ref, theirs_ref, out_ref):
@@ -265,12 +272,18 @@
     got_b = lax.ppermute(send_b, "core", SWAP)
     theirs = lax.ppermute(mine, "xh", SWAP)
 
+    whole = jax.ShapeDtypeStruct((64, PACK, TILE), jnp.bfloat16)
+    near = jax.ShapeDtypeStruct((32, PACK, TILE), jnp.bfloat16)
     outgoing = pl.pallas_call(
-        join,
-        in_specs=[vmem] * 4,
-        out_shape=jax.ShapeDtypeStruct((64, PACK, TILE), jnp.bfloat16),
-        compiler_params=params,
-    )(keep_a, got_a, keep_b, got_b)
+        join_near, in_specs=[vmem] * 2, out_specs=vmem, out_shape=near, compiler_params=params
+    )(keep_a, got_a)
+    outgoing = pl.pallas_call(
+        join_far,
+        in_specs=[vmem] * 3,
+        out_specs=vmem,
+        out_shape=whole,
+        compiler_params=params,
+    )(keep_b, got_b, outgoing)
     arrived = lax.all_to_all(outgoing, ("xl", "y", "z"), 0, 0, tiled=True)
     grad_rows = pl.pallas_call(
         functools.partial(finish_rows, 1.0 / math.sqrt(words * 256)),

time: 79.1 us -> 79.1 us (level)
  no operation moved by 1% of the time
where the time goes in v4:
time: 79.1 us; the launch traced here: 77.6 us
  waiting for transfers between devices  30.2 us (38%)
  starting transfers between devices  26.6 us (34%)
  Pallas kernels  17.2 us (22%)
  local copies, waits for them, and re-layouts  2.11 us (3%)
  between operations  1.38 us (2%)
    pallas_call x2, Pallas kernels, run_half(): pl.pallas_call(functools.partial(half_step, first), in_specs=[smem, pl.Bl...  13.1 us
    all_to_all x1, starting transfers between devices, body(): quarter = lax.all_to_all(fan_out, ('y', 'z'), 0, 0, tiled=True)  12 us
    ppermute x1, waiting for transfers between devices, body(): theirs = lax.ppermute(mine, 'xh', SWAP)  10.2 us
    all_to_all x1, waiting for transfers between devices, body(): arrived = lax.all_to_all(outgoing, ('xl', 'y', 'z'), 0, 0, tiled=True)  8.62 us
    all_to_all x1, waiting for transfers between devices, body(): quarter = lax.all_to_all(fan_out, ('y', 'z'), 0, 0, tiled=True)  8.54 us
    all_to_all x1, starting transfers between devices, body(): arrived = lax.all_to_all(outgoing, ('xl', 'y', 'z'), 0, 0, tiled=True)  5.06 us
    ppermute x1, starting transfers between devices, body(): peer = lax.ppermute(quarter, 'core', SWAP)  4.34 us
    ppermute x1, starting transfers between devices, body(): theirs = lax.ppermute(mine, 'xh', SWAP)  2.75 us
  transfers between devices with their start and end apart: 8, of which 5 were waited for; matrix products, arithmetic and copies ran while one was open for 0% of the time, Pallas kernels for 20%

profile of v4, /device:TPU:1, one launch (start us, length us, event | category | flops | bytes accessed | tf_op | source)
XLA Modules:
  0.0 77.6 jit_solution(10214089377077465380)
XLA Ops:
  0.6 0.0 copy-start
  0.6 0.0 copy-start.1
  0.7 0.0 copy-start.2
  0.7 0.8 copy-done.2
  1.4 0.0 copy-start.4
  1.4 0.7 copy-done.4
  2.1 0.9 %shard_map.86 = bf16[32,40,128]{2,1,0:T(8,128)(2,1)} custom-call(bf16[16,300]{1,0:T(8,128)(2,1)S(1)} %bitcast.11, s32[1,16]{1,0:T(1,128)S(1)} %copy-done.4), custom_call_target="tpu_custom_call" | custom-call | tf_op jit(solution)/shard_map/pallas_call | solution.py:239
  3.0 12.0 %all-to-all-start = ((bf16[32,40,128]{2,1,0:T(8,128)(2,1)}), bf16[32,40,128]{2,1,0:T(8,128)(2,1)S(1)}, u32[]{:S(2)}, u32[]{:S(2)}) async-start(bf16[32,40,128]{2,1,0:T(8,128)(2,1)} %shard_map.86), calls=%async_computation | async-start | bytes 655360 | tf_op jit(solution)/shard_map/all_to_all | solution.py:244
  15.7 0.0 copy-done
  15.7 0.0 copy-start.3
  15.7 0.7 copy-done.3
  16.4 0.3 shard_map.87
  16.6 8.5 %all-to-all-done.own_ref = bf16[32,40,128]{2,1,0:T(8,128)(2,1)S(1)} async-done(((bf16[32,40,128]{2,1,0:T(8,128)(2,1)}), bf16[32,40,128]{2,1,0:T(8,128)(2,1)S(1)}, u32[]{:S(2)}, u32[]{:S(2)}) %all-to-all-start) | async-done | bytes 327712 | tf_op jit(solution)/shard_map/all_to_all | solution.py:244
  25.2 4.3 %collective-permute-start.1 = (bf16[32,40,128]{2,1,0:T(8,128)(2,1)S(1)}, bf16[32,40,128]{2,1,0:T(8,128)(2,1)S(1)}, u32[]{:S(2)}, u32[]{:S(2)}) collective-permute-start(bf16[32,40,128]{2,1,0:T(8,128)(2,1)S(1)} %all-to-all-done.own_ref), channel_id=1, source_target_pairs={{0,2},{2,0},{1,3},{3,1},{4,6},{6,4},{5,7},{7,5},{8,10},{10,8},{9,1... | collective-permute-start | bytes 983048 | tf_op jit(solution)/shard_map/ppermute | solution.py:261
  29.5 1.2 %collective-permute-start = (bf16[32,40,128]{2,1,0:T(8,128)(2,1)S(1)}, bf16[32,40,128]{2,1,0:T(8,128)(2,1)S(1)}, u32[]{:S(2)}, u32[]{:S(2)}) collective-permute-start(bf16[32,40,128]{2,1,0:T(8,128)(2,1)S(1)} %all-to-all-done.own_ref), channel_id=1, source_target_pairs={{0,128},{128,0},{1,129},{129,1},{2,130},{130,2},{3,131},{131,3},{4... | collective-permute-start | bytes 983048 | tf_op jit(solution)/shard_map/ppermute | solution.py:262
  30.7 0.0 collective-permute-done.1.peer_ref
  30.8 0.0 copy-done.1
  30.8 6.5 %shard_map.88 = (f32[304,1024]{1,0:T(8,128)S(1)}, f32[32,40,128]{2,1,0:T(8,128)S(1)}, f32[32,40,128]{2,1,0:T(8,128)S(1)}) custom-call(s32[8,16]{1,0:T(8,128)S(1)} %bitcast.9, s32[1024,16,128]{2,1,0:T(8,128)} %bitcast.13, bf16[384,1024]{1,0:T(8,128)(2,1)S(1)} %get-tuple-element.17.wide_ref, bf16[1024,384]{1,0:T(8,128)(2,1)S(1)} %get-tuple-element.18.turned_ref, ...), custom_call_target="tpu_custom_call" | custom-call | flops 1887436800 | bytes 4194304 | tf_op jit(solution)/shard_map/pallas_call | solution.py:187
  37.3 1.6 %collective-permute-done.own_ref = bf16[32,40,128]{2,1,0:T(8,128)(2,1)S(1)} collective-permute-done((bf16[32,40,128]{2,1,0:T(8,128)(2,1)S(1)}, bf16[32,40,128]{2,1,0:T(8,128)(2,1)S(1)}, u32[]{:S(2)}, u32[]{:S(2)}) %collective-permute-start) | collective-permute-done | bytes 327712 | tf_op jit(solution)/shard_map/ppermute | solution.py:262
  38.9 0.8 %collective-permute-start.2 = (bf16[32,40,128]{2,1,0:T(8,128)(2,1)S(1)}, bf16[32,40,128]{2,1,0:T(8,128)(2,1)S(1)}, u32[]{:S(2)}, u32[]{:S(2)}) collective-permute-start(bf16[32,40,128]{2,1,0:T(8,128)(2,1)S(1)} %collective-permute-done.own_ref), channel_id=1, source_target_pairs={{0,2},{2,0},{1,3},{3,1},{4,6},{6,4},{5,7},{7,5},{8,10},{10,8},{9,1... | collective-permute-start | bytes 983048 | tf_op jit(solution)/shard_map/ppermute | solution.py:267
  39.7 0.0 collective-permute-start.5
  39.7 1.3 %collective-permute-done.2.peer_ref = bf16[32,40,128]{2,1,0:T(8,128)(2,1)S(1)} collective-permute-done((bf16[32,40,128]{2,1,0:T(8,128)(2,1)S(1)}, bf16[32,40,128]{2,1,0:T(8,128)(2,1)S(1)}, u32[]{:S(2)}, u32[]{:S(2)}) %collective-permute-start.2) | collective-permute-done | bytes 327712 | tf_op jit(solution)/shard_map/ppermute | solution.py:267
  40.9 6.6 %shard_map.89 = (bf16[304,1024]{1,0:T(8,128)(2,1)S(1)}, f32[32,40,128]{2,1,0:T(8,128)S(1)}, f32[32,40,128]{2,1,0:T(8,128)S(1)}) custom-call(s32[8,16]{1,0:T(8,128)S(1)} %bitcast.10, s32[1024,16,128]{2,1,0:T(8,128)} %bitcast.14, bf16[384,1024]{1,0:T(8,128)(2,1)S(1)} %get-tuple-element.17.wide_ref, bf16[1024,384]{1,0:T(8,128)(2,1)S(1)} %get-tuple-element.18.turned_ref, ...), custom_call_target="tpu_custom_call" | custom-call | flops 1887436800 | bytes 4194304 | tf_op jit(solution)/shard_map/pallas_call | solution.py:187
  47.5 0.5 collective-permute-start.4
  48.0 2.7 %collective-permute-start.3 = (bf16[304,1024]{1,0:T(8,128)(2,1)S(1)}, bf16[304,1024]{1,0:T(8,128)(2,1)S(1)}, u32[]{:S(2)}, u32[]{:S(2)}) collective-permute-start(bf16[304,1024]{1,0:T(8,128)(2,1)S(1)} %get-tuple-element.23.mine_ref), channel_id=1, source_target_pairs={{0,1},{1,0},{2,3},{3,2},{4,5},{5,4},{6,7},{7,6},{8,9},{9,8},{10,11... | collective-permute-start | bytes 1867784 | tf_op jit(solution)/shard_map/ppermute | solution.py:273
  50.7 0.0 collective-permute-done.5.got
  50.7 0.1 shard_map.91.near_ref
  50.8 0.0 collective-permute-done.4.got
  50.8 0.9 %shard_map.92 = bf16[64,40,128]{2,1,0:T(8,128)(2,1)} custom-call(f32[32,40,128]{2,1,0:T(8,128)S(1)} %get-tuple-element.24.keep, f32[32,40,128]{2,1,0:T(8,128)S(1)} %collective-permute-done.4.got, bf16[32,40,128]{2,1,0:T(8,128)(2,1)S(1)} %shard_map.91.near_ref), custom_call_target="tpu_custom_call" | custom-call | tf_op jit(solution)/shard_map/pallas_call | solution.py:280
  51.7 5.1 %all-to-all-start.1 = ((bf16[64,40,128]{2,1,0:T(8,128)(2,1)}), bf16[64,40,128]{2,1,0:T(8,128)(2,1)S(1)}, u32[]{:S(2)}, u32[]{:S(2)}) async-start(bf16[64,40,128]{2,1,0:T(8,128)(2,1)} %shard_map.92), calls=%async_computation.1 | async-start | bytes 1310720 | tf_op jit(solution)/shard_map/all_to_all | solution.py:287
  56.8 10.2 %collective-permute-done.3.theirs_ref = bf16[304,1024]{1,0:T(8,128)(2,1)S(1)} collective-permute-done((bf16[304,1024]{1,0:T(8,128)(2,1)S(1)}, bf16[304,1024]{1,0:T(8,128)(2,1)S(1)}, u32[]{:S(2)}, u32[]{:S(2)}) %collective-permute-start.3) | collective-permute-done | bytes 622624 | tf_op jit(solution)/shard_map/ppermute | solution.py:273
  67.0 1.2 %shard_map.90 = f32[300,1024]{1,0:T(8,128)} custom-call(bf16[304,1024]{1,0:T(8,128)(2,1)S(1)} %get-tuple-element.23.mine_ref, bf16[304,1024]{1,0:T(8,128)(2,1)S(1)} %collective-permute-done.3.theirs_ref), custom_call_target="tpu_custom_call" | custom-call | flops 99999997952 | bytes 2457600 | tf_op jit(solution)/shard_map/pallas_call | solution.py:288
  68.2 8.6 %all-to-all-done.1.got_ref = bf16[64,40,128]{2,1,0:T(8,128)(2,1)S(1)} async-done(((bf16[64,40,128]{2,1,0:T(8,128)(2,1)}), bf16[64,40,128]{2,1,0:T(8,128)(2,1)S(1)}, u32[]{:S(2)}, u32[]{:S(2)}) %all-to-all-start.1) | async-done | bytes 655392 | tf_op jit(solution)/shard_map/all_to_all | solution.py:287
  76.8 0.8 %shard_map.93 = f32[16,300]{1,0:T(8,128)} custom-call(bf16[64,40,128]{2,1,0:T(8,128)(2,1)S(1)} %all-to-all-done.1.got_ref), custom_call_target="tpu_custom_call" | custom-call | tf_op jit(solution)/shard_map/pallas_call | solution.py:296
Async XLA Ops:
  0.6 15.0 %copy-start = (bf16[300,1024]{1,0:T(8,128)(2,1)S(1)}, bf16[300,1024]{1,0:T(8,128)(2,1)}, u32[]{:S(2)}) copy-start(bf16[300,1024]{1,0:T(8,128)(2,1)} %embed_ref.1) | copy-start | bytes 1843204
  0.6 30.2 %copy-start.1 = (s32[8,1,16]{2,1,0:T(1,128)S(1)}, s32[8,1,16]{2,1,0:T(1,128)}, u32[]{:S(2)}) copy-start(s32[8,1,16]{2,1,0:T(1,128)} %param.10) | copy-start | bytes 1540
  0.7 0.8 copy-start.2
  1.4 0.7 copy-start.4
  3.0 22.2 %all-to-all-start = ((bf16[32,40,128]{2,1,0:T(8,128)(2,1)}), bf16[32,40,128]{2,1,0:T(8,128)(2,1)S(1)}, u32[]{:S(2)}, u32[]{:S(2)}) async-start(bf16[32,40,128]{2,1,0:T(8,128)(2,1)} %shard_map.86), calls=%async_computation | async-start | bytes 655360 | tf_op jit(solution)/shard_map/all_to_all | solution.py:244
  15.7 0.7 copy-start.3
  25.2 5.6 %collective-permute-start.1 = (bf16[32,40,128]{2,1,0:T(8,128)(2,1)S(1)}, bf16[32,40,128]{2,1,0:T(8,128)(2,1)S(1)}, u32[]{:S(2)}, u32[]{:S(2)}) collective-permute-start(bf16[32,40,128]{2,1,0:T(8,128)(2,1)S(1)} %all-to-all-done.own_ref), channel_id=1, source_target_pairs={{0,2},{2,0},{1,3},{3,1},{4,6},{6,4},{5,7},{7,5},{8,10},{10,8},{9,1... | collective-permute-start | bytes 983048 | tf_op jit(solution)/shard_map/ppermute | solution.py:261
  29.5 9.3 %collective-permute-start = (bf16[32,40,128]{2,1,0:T(8,128)(2,1)S(1)}, bf16[32,40,128]{2,1,0:T(8,128)(2,1)S(1)}, u32[]{:S(2)}, u32[]{:S(2)}) collective-permute-start(bf16[32,40,128]{2,1,0:T(8,128)(2,1)S(1)} %all-to-all-done.own_ref), channel_id=1, source_target_pairs={{0,128},{128,0},{1,129},{129,1},{2,130},{130,2},{3,131},{131,3},{4... | collective-permute-start | bytes 983048 | tf_op jit(solution)/shard_map/ppermute | solution.py:262
  38.9 2.0 %collective-permute-start.2 = (bf16[32,40,128]{2,1,0:T(8,128)(2,1)S(1)}, bf16[32,40,128]{2,1,0:T(8,128)(2,1)S(1)}, u32[]{:S(2)}, u32[]{:S(2)}) collective-permute-start(bf16[32,40,128]{2,1,0:T(8,128)(2,1)S(1)} %collective-permute-done.own_ref), channel_id=1, source_target_pairs={{0,2},{2,0},{1,3},{3,1},{4,6},{6,4},{5,7},{7,5},{8,10},{10,8},{9,1... | collective-permute-start | bytes 983048 | tf_op jit(solution)/shard_map/ppermute | solution.py:267
  39.7 11.1 %collective-permute-start.5 = (f32[32,40,128]{2,1,0:T(8,128)S(1)}, f32[32,40,128]{2,1,0:T(8,128)S(1)}, u32[]{:S(2)}, u32[]{:S(2)}) collective-permute-start(f32[32,40,128]{2,1,0:T(8,128)S(1)} %get-tuple-element.27), channel_id=1, source_target_pairs={{0,2},{2,0},{1,3},{3,1},{4,6},{6,4},{5,7},{7,5},{8,10},{10,8},{9,1... | collective-permute-start | bytes 1966088 | tf_op jit(solution)/shard_map/ppermute | solution.py:268
  47.5 3.3 %collective-permute-start.4 = (f32[32,40,128]{2,1,0:T(8,128)S(1)}, f32[32,40,128]{2,1,0:T(8,128)S(1)}, u32[]{:S(2)}, u32[]{:S(2)}) collective-permute-start(f32[32,40,128]{2,1,0:T(8,128)S(1)} %get-tuple-element.25), channel_id=1, source_target_pairs={{0,2},{2,0},{1,3},{3,1},{4,6},{6,4},{5,7},{7,5},{8,10},{10,8},{9,1... | collective-permute-start | bytes 1966088 | tf_op jit(solution)/shard_map/ppermute | solution.py:272
  48.0 19.0 %collective-permute-start.3 = (bf16[304,1024]{1,0:T(8,128)(2,1)S(1)}, bf16[304,1024]{1,0:T(8,128)(2,1)S(1)}, u32[]{:S(2)}, u32[]{:S(2)}) collective-permute-start(bf16[304,1024]{1,0:T(8,128)(2,1)S(1)} %get-tuple-element.23.mine_ref), channel_id=1, source_target_pairs={{0,1},{1,0},{2,3},{3,2},{4,5},{5,4},{6,7},{7,6},{8,9},{9,8},{10,11... | collective-permute-start | bytes 1867784 | tf_op jit(solution)/shard_map/ppermute | solution.py:273
  51.7 25.1 %all-to-all-start.1 = ((bf16[64,40,128]{2,1,0:T(8,128)(2,1)}), bf16[64,40,128]{2,1,0:T(8,128)(2,1)S(1)}, u32[]{:S(2)}, u32[]{:S(2)}) async-start(bf16[64,40,128]{2,1,0:T(8,128)(2,1)} %shard_map.92), calls=%async_computation.1 | async-start | bytes 1310720 | tf_op jit(solution)/shard_map/all_to_all | solution.py:287
